TPU v7x, 32 devices: a whole 2x2x4 slice. The times are simulated.
32 devices in a mesh: patch: 8 (over z, y), visit: 4 (over x, core).
Axes of the slice: x: 2, y: 2, z: 4, core: 2. Of those that a mesh axis runs over, the one named last changes fastest.
Arguments:
- pieces: bfloat16 [3072, 32, 128], P(('patch', 'visit')), may hold values from -16 to 16
- dest: int32 [3072, 1], P(('patch', 'visit')), may hold values from 0 to 7; in each aligned block of 96 rows (0 to 95, 96 to 191, ...) at most 24 rows name the same one
- offsets: int32 [3072], P(('patch', 'visit')), may hold values from 0 to 224
- kernel_index: int32 [3072], P(('patch', 'visit')), may hold values from 0 to 39
- weights: bfloat16 [3072], P(('patch', 'visit')), may hold values from 0.25 to 4
- basis_col: bfloat16 [14, 41], replicated, may hold values from -1 to 1
- basis_row: bfloat16 [14, 41], replicated, may hold values from -1 to 1
- coef_table: float32 [40, 14], replicated, may hold values from -2.4 to 2.4
- det_taps: bfloat16 [2, 21], replicated, may hold values from -1.25 to 1.25
Outputs:
- coadd: float32 [2048, 128], P(('patch', 'visit'))
- detection: float32 [2048, 128], P(('patch', 'visit'))
Inputs may be any that keep to these rules, and one draw needn't show every extreme that they name: `dest`: at most 24 of the pieces of one device intersect one patch.
All inputs are finite; a program needn't handle non-finite values.
Results may differ from a plain program's by a relative error of at most 0.0062.
Values may be sent and summed in bfloat16 or wider, within the bound.
No kernel may reach another device: no remote copies, remote signals or barrier semaphores. Data moves between devices by JAX's collectives and lax.ppermute only.
A program may use at most 64 MiB of HBM per device.

v0:
```python
from functools import partial
import math

import jax
import jax.numpy as jnp
from jax import lax
from jax.experimental import pallas as pl
from jax.experimental.pallas import tpu as pltpu
from jax.sharding import PartitionSpec as P

PH = 256
F32 = jnp.float32
BF16 = jnp.bfloat16


def iota(shape, dim):
    return lax.broadcasted_iota(jnp.int32, shape, dim)


def dot(a, b):
    return jnp.dot(a, b, preferred_element_type=F32)


def dot_nt(a, b):
    return lax.dot_general(a, b, (((1,), (1,)), ((), ())), preferred_element_type=F32)


def dot_tn(a, b):
    return lax.dot_general(a, b, (((0,), (0,)), ((), ())), preferred_element_type=F32)


def toeplitz(taps, rows, lanes, shift):
    first = pltpu.roll(jnp.broadcast_to(taps, (8, lanes)), 0, 1, stride=1, stride_axis=0)
    blocks = [pltpu.roll(first, (i + shift) % lanes, 1) for i in range(0, rows, 8)]
    return jnp.concatenate(blocks, axis=0)


def masked_bands(table, rows, lanes, shift, mask):
    padded = jnp.concatenate(
        [table, jnp.zeros((table.shape[0], lanes - table.shape[1]), F32)], axis=1
    )
    for b in range(table.shape[0]):
        yield b, jnp.where(mask, toeplitz(padded[b:b + 1], rows, lanes, shift), 0.0)


def split(x):
    high = x.astype(BF16)
    return high, (x - high.astype(F32)).astype(BF16)


def coadd_kernel(
    geometry,
    col_h, row_h, dest_h, off_h, kind_h, weight_h, coef_h, taps_h, pieces_h,
    dest_s_h, off_s_h,
    kept, sent, across, along,
    col, row, dest_v, off_v, kind_v, weight_v, coef, det_taps, pieces, dest_s, off_s,
    col_bands, row_bands, factors, even, odd, acc, den, sems,
):
    patches, strips, halo, stride, group, groups, halved = geometry
    count, height, width = pieces.shape
    basis, taps = col.shape
    half = taps // 2
    strip = PH // strips
    span = kept.shape[1]
    sources = (
        col_h, row_h, dest_h, off_h, kind_h, weight_h, coef_h, taps_h, pieces_h, dest_s_h,
        off_s_h,
    )
    targets = (
        col, row, dest_v, off_v, kind_v, weight_v, coef, det_taps, pieces, dest_s, off_s
    )
    copies = [
        pltpu.make_async_copy(source, target, sems.at[k])
        for k, (source, target) in enumerate(zip(sources, targets))
    ]
    for copy in copies:
        copy.start()
    acc[...] = jnp.zeros_like(acc)
    for copy in copies[:2]:
        copy.wait()
    x, y = iota((width, width), 1), iota((width, width), 0)
    near = jnp.abs(x - y) <= half
    for b, band in masked_bands(col[...].astype(F32), width, width, -half, near):
        col_bands[b * width:(b + 1) * width, :] = band.astype(BF16)
    near = near & (x // height == y // height)
    for b, band in masked_bands(row[...].astype(F32), width, width, -half, near):
        row_bands[b * width:(b + 1) * width, :] = band.astype(BF16)
    for copy in copies[2:]:
        copy.wait()
    table, detect = det_taps[...].astype(F32), det_taps.shape[1]
    ((_, band),) = masked_bands(table[1:2], width, width, -halo, jnp.abs(x - y) <= halo)
    across[...] = band.astype(BF16)
    diff = iota((strip, width), 1) - iota((strip, width), 0)
    ((_, band),) = masked_bands(table[0:1], strip, width, 0, (diff >= 0) & (diff < detect))
    along[...] = band.astype(BF16)
    kinds = coef.shape[1]
    weight = weight_v[...].astype(F32)
    picked = jnp.where(iota((kinds, count), 0) == kind_v[...], weight, 0.0).astype(BF16)
    high, low = split(coef[...])
    high, low = split(dot(high, picked) + dot(low, picked))
    spread = (
        iota((basis, basis * width), 1) // width == iota((basis, basis * width), 0)
    ).astype(BF16)
    factors[...] = (dot_tn(high, spread) + dot_tn(low, spread)).reshape(factors.shape)
    share = jnp.where(iota((patches, count), 0) == dest_v[...], weight, 0.0).astype(BF16)
    for v in range(strips):
        at = iota((width, count), 0) + (v * strip - halo) - off_v[...]
        covered = ((at >= 0) & (at < height)).astype(BF16)
        den[v] = dot_nt(share, covered)

    chunk, together = groups * group, 7

    def row_step(i, scaled):
        base = pl.multiple_of(i * chunk, chunk)
        images = jnp.concatenate(
            [
                pieces[pl.ds(base + g * group, group)].reshape(width, width)
                for g in range(groups)
            ],
            axis=1,
        )
        for start in range(0, basis, together):
            stop = min(start + together, basis)
            rowed = dot(row_bands[start * width:stop * width, :], images)
            for b in range(start, stop):
                at = slice(b * width, (b + 1) * width)
                for g in range(groups):
                    for j in range(group):
                        top = (b - start) * width + j * height
                        part = rowed[top:top + height, g * width:(g + 1) * width]
                        row = g * group + j
                        part = part * factors[i, row:row + 1, at]
                        first = g * width + j * height
                        scaled[first:first + height, at] = part.astype(BF16)

    def column_step(i, scaled):
        base = i * chunk
        matched = dot(scaled[...], col_bands[...])
        for j in range(chunk):
            place = pl.ds(dest_s[base + j] * stride + halo + off_s[base + j], height)
            acc[place, :] = acc[place, :] + matched[j * height:(j + 1) * height]

    chunks = count // chunk
    row_step(0, even)

    def two(k, carry):
        row_step(2 * k + 1, odd)
        column_step(2 * k, even)
        row_step(2 * k + 2, even)
        column_step(2 * k + 1, odd)
        return carry

    lax.fori_loop(0, chunks // 2 - 1, two, 0)
    row_step(chunks - 1, odd)
    column_step(chunks - 2, even)
    column_step(chunks - 1, odd)
    own = iota((span, width), 0) < strip + 2 * halo
    me = lax.axis_index("patch") * strips + lax.axis_index("visit")
    parts = patches * strips

    def strip_at(position):
        away = 0
        for stage, mask in enumerate(halving_masks(halved)):
            away = away ^ (((position >> (halved + 3 - stage)) & 1) * mask)
        for k in range(2):
            away = away ^ direct_mask(halved, k, (position >> (2 - 2 * k)) & 3)
        device = away ^ me
        p, v = device // strips, lax.rem(device, strips)
        base = pl.multiple_of(p * stride + v * strip, 8)
        return jnp.where(own, acc[pl.ds(base, span), :], den[v, pl.ds(p, 1), :])

    def finish(i, carry):
        sent[i] = strip_at(i + parts // 2).astype(BF16)
        kept[i] = strip_at(i)
        return carry

    lax.fori_loop(0, parts // 2, finish, 0, unroll=4)


def detect_kernel(halo, *refs):
    *terms, across, along, coadd, detection = refs
    span, width = terms[0].shape
    strip = coadd.shape[0]
    total = terms[0][...]
    for term in terms[1:]:
        total = total + term[...].astype(F32)
    rows = iota((span, width), 0)
    square = jnp.broadcast_to(total[strip + 2 * halo:strip + 2 * halo + 1], (width, width))
    weight = jnp.transpose(square)[:span]
    value = jnp.where(rows < strip + 2 * halo, total / (1.0 + weight), 0.0)
    coadd[...] = value[halo:halo + strip]
    columns, filt = across[...], along[...]
    high, low = split(value)
    smooth = dot(high, columns) + dot(low, columns)
    smooth = jnp.concatenate([smooth, jnp.zeros((width - span, width), F32)], axis=0)
    high, low = split(smooth)
    detection[...] = dot(filt, high) + dot(filt, low)


def halving_masks(halved):
    return [1 << k | 1 for k in range(halved)]


def direct_mask(halved, k, member):
    return (member << (halved + 2 * k)) | ((member | (member >> 1)) & 1)


def exchange(x, mask):
    parts = lax.axis_size("patch") * lax.axis_size("visit")
    return lax.ppermute(x, ("patch", "visit"), [(d, d ^ mask) for d in range(parts)])


def exchange_direct(sums, mask, order):
    return [sums[0]] + [exchange(sums[k].astype(BF16), mask(k)) for k in order]


def shards(
    pieces, dest, offsets, kernel_index, weights, basis_col, basis_row, coef_table, det_taps
):
    patches = lax.axis_size("patch")
    strips = lax.axis_size("visit")
    count, height, width = pieces.shape
    basis = basis_col.shape[0]
    halo = det_taps.shape[1] // 2
    strip = PH // strips
    span = -(-(strip + 2 * halo + 1) // 8) * 8
    stride = strip * (strips - 1) + span
    group = width // height
    groups = 4
    parts = patches * strips
    vmem = pl.BlockSpec(memory_space=pltpu.VMEM)
    inputs = (
        basis_col, basis_row, dest.reshape(1, count), offsets.reshape(1, count),
        kernel_index.reshape(1, count), weights.reshape(1, count), coef_table.T, det_taps, pieces,
        dest[:, 0], offsets,
    )
    bits = parts.bit_length() - 1
    halved = bits - 4
    shape = (parts // 2, span, width)
    shapes = [jax.ShapeDtypeStruct(shape, F32), jax.ShapeDtypeStruct(shape, BF16)]
    shapes += [jax.ShapeDtypeStruct((rows, width), BF16) for rows in (width, strip)]
    grant = 10 * 1024 * 1024 + 3 * parts * span * width + 4 * patches * stride * width
    kept, sent, across, along = pl.pallas_call(
        partial(coadd_kernel, (patches, strips, halo, stride, group, groups, halved)),
        out_shape=shapes,
        in_specs=[pl.BlockSpec(memory_space=pltpu.HBM)] * len(inputs),
        out_specs=[vmem] * 4,
        scratch_shapes=[pltpu.VMEM(x.shape, x.dtype) for x in inputs[:-2]]
        + [pltpu.SMEM(x.shape, x.dtype) for x in inputs[-2:]]
        + [
            pltpu.VMEM((basis * width, width), BF16),
            pltpu.VMEM((basis * width, width), BF16),
            pltpu.VMEM((count // (groups * group), groups * group, basis * width), F32),
            pltpu.VMEM((groups * width, basis * width), BF16),
            pltpu.VMEM((groups * width, basis * width), BF16),
            pltpu.VMEM((patches * stride, width), F32),
            pltpu.VMEM((strips, patches, width), F32),
            pltpu.SemaphoreType.DMA((len(inputs),)),
        ],
        compiler_params=pltpu.CompilerParams(vmem_limit_bytes=grant),
        name="coadd_partials",
    )(*[pltpu.with_memory_space_constraint(x, pltpu.HBM) for x in inputs])
    def exchange(x, mask):
        return lax.ppermute(x, ("patch", "visit"), [(d, d ^ mask) for d in range(parts)])

    for stage, mask in enumerate(halving_masks(halved)):
        if stage:
            left = kept.shape[0] // 2
            sent = (kept[left:] + given[left:].astype(F32)).astype(BF16)
            kept = kept[:left] + given[:left].astype(F32)
        given = exchange(sent, mask)
    sums = [kept[4 * k:4 * k + 4] + given[4 * k:4 * k + 4].astype(F32) for k in range(4)]
    terms = exchange_direct(sums, partial(direct_mask, halved, 0), (1, 3, 2))
    total = terms[0]
    for term in terms[1:]:
        total = total + term.astype(F32)
    total = [total[k] for k in range(4)]
    terms = exchange_direct(total, partial(direct_mask, halved, 1), (2, 3, 1))
    shape = jax.ShapeDtypeStruct((strip, width), F32)
    return pl.pallas_call(
        partial(detect_kernel, halo),
        out_shape=(shape, shape),
        in_specs=[vmem] * (len(terms) + 2),
        out_specs=(vmem, vmem),
        compiler_params=pltpu.CompilerParams(vmem_limit_bytes=48 * 1024 * 1024),
        name="detect_strip",
    )(*terms, across, along)


def solution(mesh):
    in_specs = (
        P(("patch", "visit"), None, None),
        P(("patch", "visit"), None),
        P(("patch", "visit")),
        P(("patch", "visit")),
        P(("patch", "visit")),
        P(),
        P(),
        P(),
        P(),
    )
    out_specs = (P(("patch", "visit"), None), P(("patch", "visit"), None))
    return jax.shard_map(shards, mesh=mesh, in_specs=in_specs, out_specs=out_specs, check_vma=False)
```

profile of v0, /device:TPU:0, one launch (start us, length us, event | category | flops | bytes accessed | tf_op | source)
XLA Modules:
  0.0 30.6 jit_solution(10366128199412329459)
XLA Ops:
  0.6 8.9 %coadd_partials.1 = (f32[16,88,128]{2,1,0:T(8,128)S(1)}, bf16[16,88,128]{2,1,0:T(8,128)(2,1)S(1)}, bf16[128,128]{1,0:T(8,128)(2,1)S(1)}, bf16[64,128]{1,0:T(8,128)(2,1)S(1)}) custom-call(bf16[14,41]{1,0:T(8,128)(2,1)} %col_h.1, bf16[14,41]{1,0:T(8,128)(2,1)} %row_h.1, s32[1,96]{1,0:T(1,128)} %bitcast.15, s32[1,96]{1,0:T(1,128)} %bitcast.17, ...), custom_call_target="tpu_custom_call" | custom-call | tf_op jit(solution)/shard_map/coadd_partials/pallas_call | solution.py:243
  9.5 0.5 %collective-permute-start = (bf16[16,88,128]{2,1,0:T(8,128)(2,1)S(1)}, bf16[16,88,128]{2,1,0:T(8,128)(2,1)S(1)}, u32[]{:S(2)}, u32[]{:S(2)}) collective-permute-start(bf16[16,88,128]{2,1,0:T(8,128)(2,1)S(1)} %get-tuple-element.7), channel_id=1, source_target_pairs={{0,1},{1,0},{2,3},{3,2},{4,5},{5,4},{6,7},{7,6},{8,9},{9,8},{10,11... | collective-permute-start | bytes 1081352 | tf_op jit(solution)/shard_map/ppermute | solution.py:264
  10.1 1.3 %collective-permute-done = bf16[16,88,128]{2,1,0:T(8,128)(2,1)S(1)} collective-permute-done((bf16[16,88,128]{2,1,0:T(8,128)(2,1)S(1)}, bf16[16,88,128]{2,1,0:T(8,128)(2,1)S(1)}, u32[]{:S(2)}, u32[]{:S(2)}) %collective-permute-start) | collective-permute-done | bytes 360480 | tf_op jit(solution)/shard_map/ppermute | solution.py:264
  11.4 0.1 add_convert_fusion.2
  11.4 2.7 %collective-permute-start.1 = (bf16[4,88,128]{2,1,0:T(8,128)(2,1)S(1)}, bf16[4,88,128]{2,1,0:T(8,128)(2,1)S(1)}, u32[]{:S(2)}, u32[]{:S(2)}) collective-permute-start(bf16[4,88,128]{2,1,0:T(8,128)(2,1)S(1)} %get-tuple-element.12), channel_id=1, source_target_pairs={{0,3},{1,2},{2,1},{3,0},{4,7},{5,6},{6,5},{7,4},{8,11},{9,10},{10,... | collective-permute-start | bytes 270344 | tf_op jit(solution)/shard_map/ppermute | solution.py:210
  14.1 1.5 %collective-permute-start.3 = (bf16[4,88,128]{2,1,0:T(8,128)(2,1)S(1)}, bf16[4,88,128]{2,1,0:T(8,128)(2,1)S(1)}, u32[]{:S(2)}, u32[]{:S(2)}) collective-permute-start(bf16[4,88,128]{2,1,0:T(8,128)(2,1)S(1)} %get-tuple-element.13), channel_id=1, source_target_pairs={{0,5},{1,4},{2,7},{3,6},{4,1},{5,0},{6,3},{7,2},{8,13},{9,12},{10,... | collective-permute-start | bytes 270344 | tf_op jit(solution)/shard_map/ppermute | solution.py:210
  15.6 0.0 collective-permute-start.2
  15.6 1.5 %collective-permute-done.1 = bf16[4,88,128]{2,1,0:T(8,128)(2,1)S(1)} collective-permute-done((bf16[4,88,128]{2,1,0:T(8,128)(2,1)S(1)}, bf16[4,88,128]{2,1,0:T(8,128)(2,1)S(1)}, u32[]{:S(2)}, u32[]{:S(2)}) %collective-permute-start.1) | collective-permute-done | bytes 90144 | tf_op jit(solution)/shard_map/ppermute | solution.py:210
  17.1 2.9 %collective-permute-done.3 = bf16[4,88,128]{2,1,0:T(8,128)(2,1)S(1)} collective-permute-done((bf16[4,88,128]{2,1,0:T(8,128)(2,1)S(1)}, bf16[4,88,128]{2,1,0:T(8,128)(2,1)S(1)}, u32[]{:S(2)}, u32[]{:S(2)}) %collective-permute-start.3) | collective-permute-done | bytes 90144 | tf_op jit(solution)/shard_map/ppermute | solution.py:210
  20.0 1.0 %collective-permute-done.2 = bf16[4,88,128]{2,1,0:T(8,128)(2,1)S(1)} collective-permute-done((bf16[4,88,128]{2,1,0:T(8,128)(2,1)S(1)}, bf16[4,88,128]{2,1,0:T(8,128)(2,1)S(1)}, u32[]{:S(2)}, u32[]{:S(2)}) %collective-permute-start.2) | collective-permute-done | bytes 90144 | tf_op jit(solution)/shard_map/ppermute | solution.py:210
  21.1 0.1 fusion
  21.2 1.4 %collective-permute-start.6 = (bf16[88,128]{1,0:T(8,128)(2,1)S(1)}, bf16[88,128]{1,0:T(8,128)(2,1)S(1)}, u32[]{:S(2)}, u32[]{:S(2)}) collective-permute-start(bf16[88,128]{1,0:T(8,128)(2,1)S(1)} %get-tuple-element.15), channel_id=1, source_target_pairs={{0,9},{1,8},{2,11},{3,10},{4,13},{5,12},{6,15},{7,14},{8,1},{9,0},... | collective-permute-start | bytes 67592 | tf_op jit(solution)/shard_map/ppermute | solution.py:210
  22.6 2.4 %collective-permute-start.5 = (bf16[88,128]{1,0:T(8,128)(2,1)S(1)}, bf16[88,128]{1,0:T(8,128)(2,1)S(1)}, u32[]{:S(2)}, u32[]{:S(2)}) collective-permute-start(bf16[88,128]{1,0:T(8,128)(2,1)S(1)} %get-tuple-element.16), channel_id=1, source_target_pairs={{0,25},{1,24},{2,27},{3,26},{4,29},{5,28},{6,31},{7,30},{8,17},{9,... | collective-permute-start | bytes 67592 | tf_op jit(solution)/shard_map/ppermute | solution.py:210
  25.0 0.1 collective-permute-start.4
  25.1 0.0 collective-permute-done.6.refs_3_
  25.1 2.5 %collective-permute-done.5.refs_2_ = bf16[88,128]{1,0:T(8,128)(2,1)S(1)} collective-permute-done((bf16[88,128]{1,0:T(8,128)(2,1)S(1)}, bf16[88,128]{1,0:T(8,128)(2,1)S(1)}, u32[]{:S(2)}, u32[]{:S(2)}) %collective-permute-start.5) | collective-permute-done | bytes 22560 | tf_op jit(solution)/shard_map/ppermute | solution.py:210
  27.6 2.0 %collective-permute-done.4.refs_1_ = bf16[88,128]{1,0:T(8,128)(2,1)S(1)} collective-permute-done((bf16[88,128]{1,0:T(8,128)(2,1)S(1)}, bf16[88,128]{1,0:T(8,128)(2,1)S(1)}, u32[]{:S(2)}, u32[]{:S(2)}) %collective-permute-start.4) | collective-permute-done | bytes 22560 | tf_op jit(solution)/shard_map/ppermute | solution.py:210
  29.6 1.0 %detect_strip.1 = (f32[64,128]{1,0:T(8,128)}, f32[64,128]{1,0:T(8,128)}) custom-call(f32[88,128]{1,0:T(8,128)S(1)} %slice_bitcast_fusion.refs_0_, bf16[88,128]{1,0:T(8,128)(2,1)S(1)} %collective-permute-done.4.refs_1_, bf16[88,128]{1,0:T(8,128)(2,1)S(1)} %collective-permute-done.5.refs_2_, bf16[88,128]{1,0:T(8,128)(2,1)S(1)} %collective-permute-done.6.refs_3_, ...), custom_call_target="tpu_custom_call" | custom-call | tf_op jit(solution)/shard_map/detect_strip/pallas_call | solution.py:280
  (2 shorter events, 0.0 us)
Async XLA Ops:
  9.5 1.8 %collective-permute-start = (bf16[16,88,128]{2,1,0:T(8,128)(2,1)S(1)}, bf16[16,88,128]{2,1,0:T(8,128)(2,1)S(1)}, u32[]{:S(2)}, u32[]{:S(2)}) collective-permute-start(bf16[16,88,128]{2,1,0:T(8,128)(2,1)S(1)} %get-tuple-element.7), channel_id=1, source_target_pairs={{0,1},{1,0},{2,3},{3,2},{4,5},{5,4},{6,7},{7,6},{8,9},{9,8},{10,11... | collective-permute-start | bytes 1081352 | tf_op jit(solution)/shard_map/ppermute | solution.py:264
  11.4 5.7 %collective-permute-start.1 = (bf16[4,88,128]{2,1,0:T(8,128)(2,1)S(1)}, bf16[4,88,128]{2,1,0:T(8,128)(2,1)S(1)}, u32[]{:S(2)}, u32[]{:S(2)}) collective-permute-start(bf16[4,88,128]{2,1,0:T(8,128)(2,1)S(1)} %get-tuple-element.12), channel_id=1, source_target_pairs={{0,3},{1,2},{2,1},{3,0},{4,7},{5,6},{6,5},{7,4},{8,11},{9,10},{10,... | collective-permute-start | bytes 270344 | tf_op jit(solution)/shard_map/ppermute | solution.py:210
  14.1 5.9 %collective-permute-start.3 = (bf16[4,88,128]{2,1,0:T(8,128)(2,1)S(1)}, bf16[4,88,128]{2,1,0:T(8,128)(2,1)S(1)}, u32[]{:S(2)}, u32[]{:S(2)}) collective-permute-start(bf16[4,88,128]{2,1,0:T(8,128)(2,1)S(1)} %get-tuple-element.13), channel_id=1, source_target_pairs={{0,5},{1,4},{2,7},{3,6},{4,1},{5,0},{6,3},{7,2},{8,13},{9,12},{10,... | collective-permute-start | bytes 270344 | tf_op jit(solution)/shard_map/ppermute | solution.py:210
  15.6 5.5 %collective-permute-start.2 = (bf16[4,88,128]{2,1,0:T(8,128)(2,1)S(1)}, bf16[4,88,128]{2,1,0:T(8,128)(2,1)S(1)}, u32[]{:S(2)}, u32[]{:S(2)}) collective-permute-start(bf16[4,88,128]{2,1,0:T(8,128)(2,1)S(1)} %get-tuple-element.14), channel_id=1, source_target_pairs={{0,7},{1,6},{2,5},{3,4},{4,3},{5,2},{6,1},{7,0},{8,15},{9,14},{10,... | collective-permute-start | bytes 270344 | tf_op jit(solution)/shard_map/ppermute | solution.py:210
  21.2 4.0 %collective-permute-start.6 = (bf16[88,128]{1,0:T(8,128)(2,1)S(1)}, bf16[88,128]{1,0:T(8,128)(2,1)S(1)}, u32[]{:S(2)}, u32[]{:S(2)}) collective-permute-start(bf16[88,128]{1,0:T(8,128)(2,1)S(1)} %get-tuple-element.15), channel_id=1, source_target_pairs={{0,9},{1,8},{2,11},{3,10},{4,13},{5,12},{6,15},{7,14},{8,1},{9,0},... | collective-permute-start | bytes 67592 | tf_op jit(solution)/shard_map/ppermute | solution.py:210
  22.6 5.0 %collective-permute-start.5 = (bf16[88,128]{1,0:T(8,128)(2,1)S(1)}, bf16[88,128]{1,0:T(8,128)(2,1)S(1)}, u32[]{:S(2)}, u32[]{:S(2)}) collective-permute-start(bf16[88,128]{1,0:T(8,128)(2,1)S(1)} %get-tuple-element.16), channel_id=1, source_target_pairs={{0,25},{1,24},{2,27},{3,26},{4,29},{5,28},{6,31},{7,30},{8,17},{9,... | collective-permute-start | bytes 67592 | tf_op jit(solution)/shard_map/ppermute | solution.py:210
  25.0 4.6 %collective-permute-start.4 = (bf16[88,128]{1,0:T(8,128)(2,1)S(1)}, bf16[88,128]{1,0:T(8,128)(2,1)S(1)}, u32[]{:S(2)}, u32[]{:S(2)}) collective-permute-start(bf16[88,128]{1,0:T(8,128)(2,1)S(1)} %get-tuple-element.17), channel_id=1, source_target_pairs={{0,17},{1,16},{2,19},{3,18},{4,21},{5,20},{6,23},{7,22},{8,25},{9,... | collective-permute-start | bytes 67592 | tf_op jit(solution)/shard_map/ppermute | solution.py:210
where the time goes:
time: 30.8 us; the launch traced here: 30.6 us
  waiting for transfers between devices  11.3 us (37%)
  Pallas kernels  9.9 us (32%)
  starting transfers between devices  8.66 us (28%)
  between operations  0.66 us (2%)
    ppermute x7, waiting for transfers between devices, exchange(): lax.ppermute(x, ('patch', 'visit'), [(d, d ^ mask) for d in range(parts)])  11.3 us
    pallas_call x1, Pallas kernels, shards(): pl.pallas_call(partial(coadd_kernel, (patches, strips, halo, stride, grou...  8.9 us
    ppermute x7, starting transfers between devices, exchange(): lax.ppermute(x, ('patch', 'visit'), [(d, d ^ mask) for d in range(parts)])  8.66 us
    pallas_call x1, Pallas kernels, shards(): pl.pallas_call(partial(detect_kernel, halo), out_shape=(shape, shape), in...  1 us
  transfers between devices with their start and end apart: 7, of which 6 were waited for; matrix products, arithmetic and copies ran while one was open for 0% of the time, Pallas kernels for 0%

commit v1 on v0

--- a/solution.py
+++ b/solution.py
@@ -226,7 +226,7 @@
     span = -(-(strip + 2 * halo + 1) // 8) * 8
     stride = strip * (strips - 1) + span
     group = width // height
-    groups = 4
+    groups = 6
     parts = patches * strips
     vmem = pl.BlockSpec(memory_space=pltpu.VMEM)
     inputs = (
@@ -239,7 +239,7 @@
     shape = (parts // 2, span, width)
     shapes = [jax.ShapeDtypeStruct(shape, F32), jax.ShapeDtypeStruct(shape, BF16)]
     shapes += [jax.ShapeDtypeStruct((rows, width), BF16) for rows in (width, strip)]
-    grant = 10 * 1024 * 1024 + 3 * parts * span * width + 4 * patches * stride * width
+    grant = 12 * 1024 * 1024 + 3 * parts * span * width + 4 * patches * stride * width
     kept, sent, across, along = pl.pallas_call(
         partial(coadd_kernel, (patches, strips, halo, stride, group, groups, halved)),
         out_shape=shapes,

time: 30.8 us -> 30.4 us (0.987)
  Pallas kernels: 9.9 us -> 9.45 us
    pallas_call x1, Pallas kernels: 8.9 us -> 8.45 us  [shards(): pl.pallas_call(partial(coadd_kernel, (patches, strips, halo, stride, grou...]
where the time goes in v1:
time: 30.4 us; the launch traced here: 30.2 us
  waiting for transfers between devices  11.3 us (37%)
  Pallas kernels  9.45 us (31%)
  starting transfers between devices  8.66 us (28%)
  between operations  0.66 us (2%)
    ppermute x7, waiting for transfers between devices, exchange(): lax.ppermute(x, ('patch', 'visit'), [(d, d ^ mask) for d in range(parts)])  11.3 us
    ppermute x7, starting transfers between devices, exchange(): lax.ppermute(x, ('patch', 'visit'), [(d, d ^ mask) for d in range(parts)])  8.66 us
    pallas_call x1, Pallas kernels, shards(): pl.pallas_call(partial(coadd_kernel, (patches, strips, halo, stride, grou...  8.45 us
    pallas_call x1, Pallas kernels, shards(): pl.pallas_call(partial(detect_kernel, halo), out_shape=(shape, shape), in...  1 us
  transfers between devices with their start and end apart: 7, of which 6 were waited for; matrix products, arithmetic and copies ran while one was open for 0% of the time, Pallas kernels for 0%

profile of v1, /device:TPU:0, one launch (start us, length us, event | category | flops | bytes accessed | tf_op | source)
XLA Modules:
  0.0 30.2 jit_solution(9328527473783099270)
XLA Ops:
  0.6 8.5 %coadd_partials.1 = (f32[16,88,128]{2,1,0:T(8,128)S(1)}, bf16[16,88,128]{2,1,0:T(8,128)(2,1)S(1)}, bf16[128,128]{1,0:T(8,128)(2,1)S(1)}, bf16[64,128]{1,0:T(8,128)(2,1)S(1)}) custom-call(bf16[14,41]{1,0:T(8,128)(2,1)} %col_h.1, bf16[14,41]{1,0:T(8,128)(2,1)} %row_h.1, s32[1,96]{1,0:T(1,128)} %bitcast.15, s32[1,96]{1,0:T(1,128)} %bitcast.17, ...), custom_call_target="tpu_custom_call" | custom-call | tf_op jit(solution)/shard_map/coadd_partials/pallas_call | solution.py:243
  9.1 0.5 %collective-permute-start = (bf16[16,88,128]{2,1,0:T(8,128)(2,1)S(1)}, bf16[16,88,128]{2,1,0:T(8,128)(2,1)S(1)}, u32[]{:S(2)}, u32[]{:S(2)}) collective-permute-start(bf16[16,88,128]{2,1,0:T(8,128)(2,1)S(1)} %get-tuple-element.7), channel_id=1, source_target_pairs={{0,1},{1,0},{2,3},{3,2},{4,5},{5,4},{6,7},{7,6},{8,9},{9,8},{10,11... | collective-permute-start | bytes 1081352 | tf_op jit(solution)/shard_map/ppermute | solution.py:264
  9.6 1.3 %collective-permute-done = bf16[16,88,128]{2,1,0:T(8,128)(2,1)S(1)} collective-permute-done((bf16[16,88,128]{2,1,0:T(8,128)(2,1)S(1)}, bf16[16,88,128]{2,1,0:T(8,128)(2,1)S(1)}, u32[]{:S(2)}, u32[]{:S(2)}) %collective-permute-start) | collective-permute-done | bytes 360480 | tf_op jit(solution)/shard_map/ppermute | solution.py:264
  10.9 0.1 add_convert_fusion.2
  11.0 2.7 %collective-permute-start.1 = (bf16[4,88,128]{2,1,0:T(8,128)(2,1)S(1)}, bf16[4,88,128]{2,1,0:T(8,128)(2,1)S(1)}, u32[]{:S(2)}, u32[]{:S(2)}) collective-permute-start(bf16[4,88,128]{2,1,0:T(8,128)(2,1)S(1)} %get-tuple-element.12), channel_id=1, source_target_pairs={{0,3},{1,2},{2,1},{3,0},{4,7},{5,6},{6,5},{7,4},{8,11},{9,10},{10,... | collective-permute-start | bytes 270344 | tf_op jit(solution)/shard_map/ppermute | solution.py:210
  13.7 1.5 %collective-permute-start.3 = (bf16[4,88,128]{2,1,0:T(8,128)(2,1)S(1)}, bf16[4,88,128]{2,1,0:T(8,128)(2,1)S(1)}, u32[]{:S(2)}, u32[]{:S(2)}) collective-permute-start(bf16[4,88,128]{2,1,0:T(8,128)(2,1)S(1)} %get-tuple-element.13), channel_id=1, source_target_pairs={{0,5},{1,4},{2,7},{3,6},{4,1},{5,0},{6,3},{7,2},{8,13},{9,12},{10,... | collective-permute-start | bytes 270344 | tf_op jit(solution)/shard_map/ppermute | solution.py:210
  15.2 0.0 collective-permute-start.2
  15.2 1.5 %collective-permute-done.1 = bf16[4,88,128]{2,1,0:T(8,128)(2,1)S(1)} collective-permute-done((bf16[4,88,128]{2,1,0:T(8,128)(2,1)S(1)}, bf16[4,88,128]{2,1,0:T(8,128)(2,1)S(1)}, u32[]{:S(2)}, u32[]{:S(2)}) %collective-permute-start.1) | collective-permute-done | bytes 90144 | tf_op jit(solution)/shard_map/ppermute | solution.py:210
  16.7 2.9 %collective-permute-done.3 = bf16[4,88,128]{2,1,0:T(8,128)(2,1)S(1)} collective-permute-done((bf16[4,88,128]{2,1,0:T(8,128)(2,1)S(1)}, bf16[4,88,128]{2,1,0:T(8,128)(2,1)S(1)}, u32[]{:S(2)}, u32[]{:S(2)}) %collective-permute-start.3) | collective-permute-done | bytes 90144 | tf_op jit(solution)/shard_map/ppermute | solution.py:210
  19.6 1.0 %collective-permute-done.2 = bf16[4,88,128]{2,1,0:T(8,128)(2,1)S(1)} collective-permute-done((bf16[4,88,128]{2,1,0:T(8,128)(2,1)S(1)}, bf16[4,88,128]{2,1,0:T(8,128)(2,1)S(1)}, u32[]{:S(2)}, u32[]{:S(2)}) %collective-permute-start.2) | collective-permute-done | bytes 90144 | tf_op jit(solution)/shard_map/ppermute | solution.py:210
  20.6 0.1 fusion
  20.7 1.4 %collective-permute-start.6 = (bf16[88,128]{1,0:T(8,128)(2,1)S(1)}, bf16[88,128]{1,0:T(8,128)(2,1)S(1)}, u32[]{:S(2)}, u32[]{:S(2)}) collective-permute-start(bf16[88,128]{1,0:T(8,128)(2,1)S(1)} %get-tuple-element.15), channel_id=1, source_target_pairs={{0,9},{1,8},{2,11},{3,10},{4,13},{5,12},{6,15},{7,14},{8,1},{9,0},... | collective-permute-start | bytes 67592 | tf_op jit(solution)/shard_map/ppermute | solution.py:210
  22.1 2.4 %collective-permute-start.5 = (bf16[88,128]{1,0:T(8,128)(2,1)S(1)}, bf16[88,128]{1,0:T(8,128)(2,1)S(1)}, u32[]{:S(2)}, u32[]{:S(2)}) collective-permute-start(bf16[88,128]{1,0:T(8,128)(2,1)S(1)} %get-tuple-element.16), channel_id=1, source_target_pairs={{0,25},{1,24},{2,27},{3,26},{4,29},{5,28},{6,31},{7,30},{8,17},{9,... | collective-permute-start | bytes 67592 | tf_op jit(solution)/shard_map/ppermute | solution.py:210
  24.6 0.1 collective-permute-start.4
  24.7 0.0 collective-permute-done.6.refs_3_
  24.7 2.5 %collective-permute-done.5.refs_2_ = bf16[88,128]{1,0:T(8,128)(2,1)S(1)} collective-permute-done((bf16[88,128]{1,0:T(8,128)(2,1)S(1)}, bf16[88,128]{1,0:T(8,128)(2,1)S(1)}, u32[]{:S(2)}, u32[]{:S(2)}) %collective-permute-start.5) | collective-permute-done | bytes 22560 | tf_op jit(solution)/shard_map/ppermute | solution.py:210
  27.2 2.1 %collective-permute-done.4.refs_1_ = bf16[88,128]{1,0:T(8,128)(2,1)S(1)} collective-permute-done((bf16[88,128]{1,0:T(8,128)(2,1)S(1)}, bf16[88,128]{1,0:T(8,128)(2,1)S(1)}, u32[]{:S(2)}, u32[]{:S(2)}) %collective-permute-start.4) | collective-permute-done | bytes 22560 | tf_op jit(solution)/shard_map/ppermute | solution.py:210
  29.2 1.0 %detect_strip.1 = (f32[64,128]{1,0:T(8,128)}, f32[64,128]{1,0:T(8,128)}) custom-call(f32[88,128]{1,0:T(8,128)S(1)} %slice_bitcast_fusion.refs_0_, bf16[88,128]{1,0:T(8,128)(2,1)S(1)} %collective-permute-done.4.refs_1_, bf16[88,128]{1,0:T(8,128)(2,1)S(1)} %collective-permute-done.5.refs_2_, bf16[88,128]{1,0:T(8,128)(2,1)S(1)} %collective-permute-done.6.refs_3_, ...), custom_call_target="tpu_custom_call" | custom-call | tf_op jit(solution)/shard_map/detect_strip/pallas_call | solution.py:280
  (2 shorter events, 0.0 us)
Async XLA Ops:
  9.1 1.8 %collective-permute-start = (bf16[16,88,128]{2,1,0:T(8,128)(2,1)S(1)}, bf16[16,88,128]{2,1,0:T(8,128)(2,1)S(1)}, u32[]{:S(2)}, u32[]{:S(2)}) collective-permute-start(bf16[16,88,128]{2,1,0:T(8,128)(2,1)S(1)} %get-tuple-element.7), channel_id=1, source_target_pairs={{0,1},{1,0},{2,3},{3,2},{4,5},{5,4},{6,7},{7,6},{8,9},{9,8},{10,11... | collective-permute-start | bytes 1081352 | tf_op jit(solution)/shard_map/ppermute | solution.py:264
  11.0 5.7 %collective-permute-start.1 = (bf16[4,88,128]{2,1,0:T(8,128)(2,1)S(1)}, bf16[4,88,128]{2,1,0:T(8,128)(2,1)S(1)}, u32[]{:S(2)}, u32[]{:S(2)}) collective-permute-start(bf16[4,88,128]{2,1,0:T(8,128)(2,1)S(1)} %get-tuple-element.12), channel_id=1, source_target_pairs={{0,3},{1,2},{2,1},{3,0},{4,7},{5,6},{6,5},{7,4},{8,11},{9,10},{10,... | collective-permute-start | bytes 270344 | tf_op jit(solution)/shard_map/ppermute | solution.py:210
  13.7 5.9 %collective-permute-start.3 = (bf16[4,88,128]{2,1,0:T(8,128)(2,1)S(1)}, bf16[4,88,128]{2,1,0:T(8,128)(2,1)S(1)}, u32[]{:S(2)}, u32[]{:S(2)}) collective-permute-start(bf16[4,88,128]{2,1,0:T(8,128)(2,1)S(1)} %get-tuple-element.13), channel_id=1, source_target_pairs={{0,5},{1,4},{2,7},{3,6},{4,1},{5,0},{6,3},{7,2},{8,13},{9,12},{10,... | collective-permute-start | bytes 270344 | tf_op jit(solution)/shard_map/ppermute | solution.py:210
  15.2 5.5 %collective-permute-start.2 = (bf16[4,88,128]{2,1,0:T(8,128)(2,1)S(1)}, bf16[4,88,128]{2,1,0:T(8,128)(2,1)S(1)}, u32[]{:S(2)}, u32[]{:S(2)}) collective-permute-start(bf16[4,88,128]{2,1,0:T(8,128)(2,1)S(1)} %get-tuple-element.14), channel_id=1, source_target_pairs={{0,7},{1,6},{2,5},{3,4},{4,3},{5,2},{6,1},{7,0},{8,15},{9,14},{10,... | collective-permute-start | bytes 270344 | tf_op jit(solution)/shard_map/ppermute | solution.py:210
  20.7 4.0 %collective-permute-start.6 = (bf16[88,128]{1,0:T(8,128)(2,1)S(1)}, bf16[88,128]{1,0:T(8,128)(2,1)S(1)}, u32[]{:S(2)}, u32[]{:S(2)}) collective-permute-start(bf16[88,128]{1,0:T(8,128)(2,1)S(1)} %get-tuple-element.15), channel_id=1, source_target_pairs={{0,9},{1,8},{2,11},{3,10},{4,13},{5,12},{6,15},{7,14},{8,1},{9,0},... | collective-permute-start | bytes 67592 | tf_op jit(solution)/shard_map/ppermute | solution.py:210
  22.1 5.0 %collective-permute-start.5 = (bf16[88,128]{1,0:T(8,128)(2,1)S(1)}, bf16[88,128]{1,0:T(8,128)(2,1)S(1)}, u32[]{:S(2)}, u32[]{:S(2)}) collective-permute-start(bf16[88,128]{1,0:T(8,128)(2,1)S(1)} %get-tuple-element.16), channel_id=1, source_target_pairs={{0,25},{1,24},{2,27},{3,26},{4,29},{5,28},{6,31},{7,30},{8,17},{9,... | collective-permute-start | bytes 67592 | tf_op jit(solution)/shard_map/ppermute | solution.py:210
  24.6 4.6 %collective-permute-start.4 = (bf16[88,128]{1,0:T(8,128)(2,1)S(1)}, bf16[88,128]{1,0:T(8,128)(2,1)S(1)}, u32[]{:S(2)}, u32[]{:S(2)}) collective-permute-start(bf16[88,128]{1,0:T(8,128)(2,1)S(1)} %get-tuple-element.17), channel_id=1, source_target_pairs={{0,17},{1,16},{2,19},{3,18},{4,21},{5,20},{6,23},{7,22},{8,25},{9,... | collective-permute-start | bytes 67592 | tf_op jit(solution)/shard_map/ppermute | solution.py:210

commit v2 on v1

--- a/solution.py
+++ b/solution.py
@@ -108,7 +108,7 @@
         covered = ((at >= 0) & (at < height)).astype(BF16)
         den[v] = dot_nt(share, covered)
 
-    chunk, together = groups * group, 7
+    chunk, together = groups * group, 2
 
     def row_step(i, scaled):
         base = pl.multiple_of(i * chunk, chunk)
@@ -150,7 +150,8 @@
         column_step(2 * k + 1, odd)
         return carry
 
-    lax.fori_loop(0, chunks // 2 - 1, two, 0)
+    if chunks > 2:
+        lax.fori_loop(0, chunks // 2 - 1, two, 0)
     row_step(chunks - 1, odd)
     column_step(chunks - 2, even)
     column_step(chunks - 1, odd)
@@ -174,7 +175,11 @@
         kept[i] = strip_at(i)
         return carry
 
-    lax.fori_loop(0, parts // 2, finish, 0, unroll=4)
+    if parts <= 32:
+        for i in range(parts // 2):
+            finish(i, 0)
+    else:
+        lax.fori_loop(0, parts // 2, finish, 0, unroll=4)
 
 
 def detect_kernel(halo, *refs):
@@ -226,7 +231,7 @@
     span = -(-(strip + 2 * halo + 1) // 8) * 8
     stride = strip * (strips - 1) + span
     group = width // height
-    groups = 6
+    groups = 12
     parts = patches * strips
     vmem = pl.BlockSpec(memory_space=pltpu.VMEM)
     inputs = (
@@ -239,7 +244,7 @@
     shape = (parts // 2, span, width)
     shapes = [jax.ShapeDtypeStruct(shape, F32), jax.ShapeDtypeStruct(shape, BF16)]
     shapes += [jax.ShapeDtypeStruct((rows, width), BF16) for rows in (width, strip)]
-    grant = 12 * 1024 * 1024 + 3 * parts * span * width + 4 * patches * stride * width
+    grant = 24 * 1024 * 1024 + 3 * parts * span * width + 4 * patches * stride * width
     kept, sent, across, along = pl.pallas_call(
         partial(coadd_kernel, (patches, strips, halo, stride, group, groups, halved)),
         out_shape=shapes,

time: 30.4 us -> 30.2 us (level)
  no operation moved by 1% of the time
where the time goes in v2:
time: 30.2 us; the launch traced here: 30 us
  waiting for transfers between devices  11.3 us (37%)
  Pallas kernels  9.25 us (31%)
  starting transfers between devices  8.64 us (29%)
  between operations  0.66 us (2%)
    ppermute x7, waiting for transfers between devices, exchange(): lax.ppermute(x, ('patch', 'visit'), [(d, d ^ mask) for d in range(parts)])  11.3 us
    ppermute x7, starting transfers between devices, exchange(): lax.ppermute(x, ('patch', 'visit'), [(d, d ^ mask) for d in range(parts)])  8.64 us
    pallas_call x1, Pallas kernels, shards(): pl.pallas_call(partial(coadd_kernel, (patches, strips, halo, stride, grou...  8.25 us
    pallas_call x1, Pallas kernels, shards(): pl.pallas_call(partial(detect_kernel, halo), out_shape=(shape, shape), in...  1 us
  transfers between devices with their start and end apart: 7, of which 6 were waited for; matrix products, arithmetic and copies ran while one was open for 0% of the time, Pallas kernels for 0%

profile of v2, /device:TPU:0, one launch (start us, length us, event | category | flops | bytes accessed | tf_op | source)
XLA Modules:
  0.0 30.0 jit_solution(14382682725595822713)
XLA Ops:
  0.6 8.3 %coadd_partials.1 = (f32[16,88,128]{2,1,0:T(8,128)S(1)}, bf16[16,88,128]{2,1,0:T(8,128)(2,1)S(1)}, bf16[128,128]{1,0:T(8,128)(2,1)S(1)}, bf16[64,128]{1,0:T(8,128)(2,1)S(1)}) custom-call(bf16[14,41]{1,0:T(8,128)(2,1)} %col_h.1, bf16[14,41]{1,0:T(8,128)(2,1)} %row_h.1, s32[1,96]{1,0:T(1,128)} %bitcast.15, s32[1,96]{1,0:T(1,128)} %bitcast.17, ...), custom_call_target="tpu_custom_call" | custom-call | tf_op jit(solution)/shard_map/coadd_partials/pallas_call | solution.py:248
  8.9 0.5 %collective-permute-start = (bf16[16,88,128]{2,1,0:T(8,128)(2,1)S(1)}, bf16[16,88,128]{2,1,0:T(8,128)(2,1)S(1)}, u32[]{:S(2)}, u32[]{:S(2)}) collective-permute-start(bf16[16,88,128]{2,1,0:T(8,128)(2,1)S(1)} %get-tuple-element.7), channel_id=1, source_target_pairs={{0,1},{1,0},{2,3},{3,2},{4,5},{5,4},{6,7},{7,6},{8,9},{9,8},{10,11... | collective-permute-start | bytes 1081352 | tf_op jit(solution)/shard_map/ppermute | solution.py:269
  9.4 1.3 %collective-permute-done = bf16[16,88,128]{2,1,0:T(8,128)(2,1)S(1)} collective-permute-done((bf16[16,88,128]{2,1,0:T(8,128)(2,1)S(1)}, bf16[16,88,128]{2,1,0:T(8,128)(2,1)S(1)}, u32[]{:S(2)}, u32[]{:S(2)}) %collective-permute-start) | collective-permute-done | bytes 360480 | tf_op jit(solution)/shard_map/ppermute | solution.py:269
  10.7 0.1 add_convert_fusion.2
  10.8 2.7 %collective-permute-start.1 = (bf16[4,88,128]{2,1,0:T(8,128)(2,1)S(1)}, bf16[4,88,128]{2,1,0:T(8,128)(2,1)S(1)}, u32[]{:S(2)}, u32[]{:S(2)}) collective-permute-start(bf16[4,88,128]{2,1,0:T(8,128)(2,1)S(1)} %get-tuple-element.12), channel_id=1, source_target_pairs={{0,3},{1,2},{2,1},{3,0},{4,7},{5,6},{6,5},{7,4},{8,11},{9,10},{10,... | collective-permute-start | bytes 270344 | tf_op jit(solution)/shard_map/ppermute | solution.py:215
  13.4 1.5 %collective-permute-start.3 = (bf16[4,88,128]{2,1,0:T(8,128)(2,1)S(1)}, bf16[4,88,128]{2,1,0:T(8,128)(2,1)S(1)}, u32[]{:S(2)}, u32[]{:S(2)}) collective-permute-start(bf16[4,88,128]{2,1,0:T(8,128)(2,1)S(1)} %get-tuple-element.13), channel_id=1, source_target_pairs={{0,5},{1,4},{2,7},{3,6},{4,1},{5,0},{6,3},{7,2},{8,13},{9,12},{10,... | collective-permute-start | bytes 270344 | tf_op jit(solution)/shard_map/ppermute | solution.py:215
  15.0 0.0 collective-permute-start.2
  15.0 1.5 %collective-permute-done.1 = bf16[4,88,128]{2,1,0:T(8,128)(2,1)S(1)} collective-permute-done((bf16[4,88,128]{2,1,0:T(8,128)(2,1)S(1)}, bf16[4,88,128]{2,1,0:T(8,128)(2,1)S(1)}, u32[]{:S(2)}, u32[]{:S(2)}) %collective-permute-start.1) | collective-permute-done | bytes 90144 | tf_op jit(solution)/shard_map/ppermute | solution.py:215
  16.5 2.9 %collective-permute-done.3 = bf16[4,88,128]{2,1,0:T(8,128)(2,1)S(1)} collective-permute-done((bf16[4,88,128]{2,1,0:T(8,128)(2,1)S(1)}, bf16[4,88,128]{2,1,0:T(8,128)(2,1)S(1)}, u32[]{:S(2)}, u32[]{:S(2)}) %collective-permute-start.3) | collective-permute-done | bytes 90144 | tf_op jit(solution)/shard_map/ppermute | solution.py:215
  19.4 1.0 %collective-permute-done.2 = bf16[4,88,128]{2,1,0:T(8,128)(2,1)S(1)} collective-permute-done((bf16[4,88,128]{2,1,0:T(8,128)(2,1)S(1)}, bf16[4,88,128]{2,1,0:T(8,128)(2,1)S(1)}, u32[]{:S(2)}, u32[]{:S(2)}) %collective-permute-start.2) | collective-permute-done | bytes 90144 | tf_op jit(solution)/shard_map/ppermute | solution.py:215
  20.4 0.1 fusion
  20.5 1.4 %collective-permute-start.6 = (bf16[88,128]{1,0:T(8,128)(2,1)S(1)}, bf16[88,128]{1,0:T(8,128)(2,1)S(1)}, u32[]{:S(2)}, u32[]{:S(2)}) collective-permute-start(bf16[88,128]{1,0:T(8,128)(2,1)S(1)} %get-tuple-element.15), channel_id=1, source_target_pairs={{0,9},{1,8},{2,11},{3,10},{4,13},{5,12},{6,15},{7,14},{8,1},{9,0},... | collective-permute-start | bytes 67592 | tf_op jit(solution)/shard_map/ppermute | solution.py:215
  21.9 2.4 %collective-permute-start.5 = (bf16[88,128]{1,0:T(8,128)(2,1)S(1)}, bf16[88,128]{1,0:T(8,128)(2,1)S(1)}, u32[]{:S(2)}, u32[]{:S(2)}) collective-permute-start(bf16[88,128]{1,0:T(8,128)(2,1)S(1)} %get-tuple-element.16), channel_id=1, source_target_pairs={{0,25},{1,24},{2,27},{3,26},{4,29},{5,28},{6,31},{7,30},{8,17},{9,... | collective-permute-start | bytes 67592 | tf_op jit(solution)/shard_map/ppermute | solution.py:215
  24.4 0.1 collective-permute-start.4
  24.5 0.0 collective-permute-done.6.refs_3_
  24.5 2.5 %collective-permute-done.5.refs_2_ = bf16[88,128]{1,0:T(8,128)(2,1)S(1)} collective-permute-done((bf16[88,128]{1,0:T(8,128)(2,1)S(1)}, bf16[88,128]{1,0:T(8,128)(2,1)S(1)}, u32[]{:S(2)}, u32[]{:S(2)}) %collective-permute-start.5) | collective-permute-done | bytes 22560 | tf_op jit(solution)/shard_map/ppermute | solution.py:215
  26.9 2.0 %collective-permute-done.4.refs_1_ = bf16[88,128]{1,0:T(8,128)(2,1)S(1)} collective-permute-done((bf16[88,128]{1,0:T(8,128)(2,1)S(1)}, bf16[88,128]{1,0:T(8,128)(2,1)S(1)}, u32[]{:S(2)}, u32[]{:S(2)}) %collective-permute-start.4) | collective-permute-done | bytes 22560 | tf_op jit(solution)/shard_map/ppermute | solution.py:215
  29.0 1.0 %detect_strip.1 = (f32[64,128]{1,0:T(8,128)}, f32[64,128]{1,0:T(8,128)}) custom-call(f32[88,128]{1,0:T(8,128)S(1)} %slice_bitcast_fusion.refs_0_, bf16[88,128]{1,0:T(8,128)(2,1)S(1)} %collective-permute-done.4.refs_1_, bf16[88,128]{1,0:T(8,128)(2,1)S(1)} %collective-permute-done.5.refs_2_, bf16[88,128]{1,0:T(8,128)(2,1)S(1)} %collective-permute-done.6.refs_3_, ...), custom_call_target="tpu_custom_call" | custom-call | tf_op jit(solution)/shard_map/detect_strip/pallas_call | solution.py:285
  (2 shorter events, 0.0 us)
Async XLA Ops:
  8.9 1.8 %collective-permute-start = (bf16[16,88,128]{2,1,0:T(8,128)(2,1)S(1)}, bf16[16,88,128]{2,1,0:T(8,128)(2,1)S(1)}, u32[]{:S(2)}, u32[]{:S(2)}) collective-permute-start(bf16[16,88,128]{2,1,0:T(8,128)(2,1)S(1)} %get-tuple-element.7), channel_id=1, source_target_pairs={{0,1},{1,0},{2,3},{3,2},{4,5},{5,4},{6,7},{7,6},{8,9},{9,8},{10,11... | collective-permute-start | bytes 1081352 | tf_op jit(solution)/shard_map/ppermute | solution.py:269
  10.8 5.7 %collective-permute-start.1 = (bf16[4,88,128]{2,1,0:T(8,128)(2,1)S(1)}, bf16[4,88,128]{2,1,0:T(8,128)(2,1)S(1)}, u32[]{:S(2)}, u32[]{:S(2)}) collective-permute-start(bf16[4,88,128]{2,1,0:T(8,128)(2,1)S(1)} %get-tuple-element.12), channel_id=1, source_target_pairs={{0,3},{1,2},{2,1},{3,0},{4,7},{5,6},{6,5},{7,4},{8,11},{9,10},{10,... | collective-permute-start | bytes 270344 | tf_op jit(solution)/shard_map/ppermute | solution.py:215
  13.4 5.9 %collective-permute-start.3 = (bf16[4,88,128]{2,1,0:T(8,128)(2,1)S(1)}, bf16[4,88,128]{2,1,0:T(8,128)(2,1)S(1)}, u32[]{:S(2)}, u32[]{:S(2)}) collective-permute-start(bf16[4,88,128]{2,1,0:T(8,128)(2,1)S(1)} %get-tuple-element.13), channel_id=1, source_target_pairs={{0,5},{1,4},{2,7},{3,6},{4,1},{5,0},{6,3},{7,2},{8,13},{9,12},{10,... | collective-permute-start | bytes 270344 | tf_op jit(solution)/shard_map/ppermute | solution.py:215
  15.0 5.5 %collective-permute-start.2 = (bf16[4,88,128]{2,1,0:T(8,128)(2,1)S(1)}, bf16[4,88,128]{2,1,0:T(8,128)(2,1)S(1)}, u32[]{:S(2)}, u32[]{:S(2)}) collective-permute-start(bf16[4,88,128]{2,1,0:T(8,128)(2,1)S(1)} %get-tuple-element.14), channel_id=1, source_target_pairs={{0,7},{1,6},{2,5},{3,4},{4,3},{5,2},{6,1},{7,0},{8,15},{9,14},{10,... | collective-permute-start | bytes 270344 | tf_op jit(solution)/shard_map/ppermute | solution.py:215
  20.5 4.0 %collective-permute-start.6 = (bf16[88,128]{1,0:T(8,128)(2,1)S(1)}, bf16[88,128]{1,0:T(8,128)(2,1)S(1)}, u32[]{:S(2)}, u32[]{:S(2)}) collective-permute-start(bf16[88,128]{1,0:T(8,128)(2,1)S(1)} %get-tuple-element.15), channel_id=1, source_target_pairs={{0,9},{1,8},{2,11},{3,10},{4,13},{5,12},{6,15},{7,14},{8,1},{9,0},... | collective-permute-start | bytes 67592 | tf_op jit(solution)/shard_map/ppermute | solution.py:215
  21.9 5.0 %collective-permute-start.5 = (bf16[88,128]{1,0:T(8,128)(2,1)S(1)}, bf16[88,128]{1,0:T(8,128)(2,1)S(1)}, u32[]{:S(2)}, u32[]{:S(2)}) collective-permute-start(bf16[88,128]{1,0:T(8,128)(2,1)S(1)} %get-tuple-element.16), channel_id=1, source_target_pairs={{0,25},{1,24},{2,27},{3,26},{4,29},{5,28},{6,31},{7,30},{8,17},{9,... | collective-permute-start | bytes 67592 | tf_op jit(solution)/shard_map/ppermute | solution.py:215
  24.4 4.6 %collective-permute-start.4 = (bf16[88,128]{1,0:T(8,128)(2,1)S(1)}, bf16[88,128]{1,0:T(8,128)(2,1)S(1)}, u32[]{:S(2)}, u32[]{:S(2)}) collective-permute-start(bf16[88,128]{1,0:T(8,128)(2,1)S(1)} %get-tuple-element.17), channel_id=1, source_target_pairs={{0,17},{1,16},{2,19},{3,18},{4,21},{5,20},{6,23},{7,22},{8,25},{9,... | collective-permute-start | bytes 67592 | tf_op jit(solution)/shard_map/ppermute | solution.py:215

commit v3 on v2

--- a/solution.py
+++ b/solution.py
@@ -56,7 +56,7 @@
     col, row, dest_v, off_v, kind_v, weight_v, coef, det_taps, pieces, dest_s, off_s,
     col_bands, row_bands, factors, even, odd, acc, den, sems,
 ):
-    patches, strips, halo, stride, group, groups, halved = geometry
+    patches, strips, halo, stride, group, chunks, halved = geometry
     count, height, width = pieces.shape
     basis, taps = col.shape
     half = taps // 2
@@ -101,20 +101,19 @@
     spread = (
         iota((basis, basis * width), 1) // width == iota((basis, basis * width), 0)
     ).astype(BF16)
-    factors[...] = (dot_tn(high, spread) + dot_tn(low, spread)).reshape(factors.shape)
+    factors[...] = dot_tn(high, spread) + dot_tn(low, spread)
     share = jnp.where(iota((patches, count), 0) == dest_v[...], weight, 0.0).astype(BF16)
     for v in range(strips):
         at = iota((width, count), 0) + (v * strip - halo) - off_v[...]
         covered = ((at >= 0) & (at < height)).astype(BF16)
         den[v] = dot_nt(share, covered)
 
-    chunk, together = groups * group, 2
-
-    def row_step(i, scaled):
-        base = pl.multiple_of(i * chunk, chunk)
+    together = 2
+
+    def row_step(base, groups, scaled):
         images = jnp.concatenate(
             [
-                pieces[pl.ds(base + g * group, group)].reshape(width, width)
+                pieces[base + g * group:base + (g + 1) * group].reshape(width, width)
                 for g in range(groups)
             ],
             axis=1,
@@ -128,33 +127,25 @@
                     for j in range(group):
                         top = (b - start) * width + j * height
                         part = rowed[top:top + height, g * width:(g + 1) * width]
-                        row = g * group + j
-                        part = part * factors[i, row:row + 1, at]
+                        n = base + g * group + j
+                        part = part * factors[n:n + 1, at]
                         first = g * width + j * height
                         scaled[first:first + height, at] = part.astype(BF16)
 
-    def column_step(i, scaled):
-        base = i * chunk
-        matched = dot(scaled[...], col_bands[...])
-        for j in range(chunk):
+    def column_step(base, groups, scaled):
+        matched = dot(scaled[:groups * width, :], col_bands[...])
+        for j in range(groups * group):
             place = pl.ds(dest_s[base + j] * stride + halo + off_s[base + j], height)
             acc[place, :] = acc[place, :] + matched[j * height:(j + 1) * height]
 
-    chunks = count // chunk
-    row_step(0, even)
-
-    def two(k, carry):
-        row_step(2 * k + 1, odd)
-        column_step(2 * k, even)
-        row_step(2 * k + 2, even)
-        column_step(2 * k + 1, odd)
-        return carry
-
-    if chunks > 2:
-        lax.fori_loop(0, chunks // 2 - 1, two, 0)
-    row_step(chunks - 1, odd)
-    column_step(chunks - 2, even)
-    column_step(chunks - 1, odd)
+    base, before = 0, None
+    for k, groups in enumerate(chunks):
+        now = (base, groups, (even, odd)[k % 2])
+        row_step(*now)
+        if before:
+            column_step(*before)
+        base, before = base + groups * group, now
+    column_step(*before)
     own = iota((span, width), 0) < strip + 2 * halo
     me = lax.axis_index("patch") * strips + lax.axis_index("visit")
     parts = patches * strips
@@ -231,7 +222,10 @@
     span = -(-(strip + 2 * halo + 1) // 8) * 8
     stride = strip * (strips - 1) + span
     group = width // height
-    groups = 12
+    chunks, left = [], count // group
+    while left:
+        chunks.append(min(left, max(2, (left * 5 + 11) // 12)))
+        left = left - chunks[-1]
     parts = patches * strips
     vmem = pl.BlockSpec(memory_space=pltpu.VMEM)
     inputs = (
@@ -246,7 +240,7 @@
     shapes += [jax.ShapeDtypeStruct((rows, width), BF16) for rows in (width, strip)]
     grant = 24 * 1024 * 1024 + 3 * parts * span * width + 4 * patches * stride * width
     kept, sent, across, along = pl.pallas_call(
-        partial(coadd_kernel, (patches, strips, halo, stride, group, groups, halved)),
+        partial(coadd_kernel, (patches, strips, halo, stride, group, chunks, halved)),
         out_shape=shapes,
         in_specs=[pl.BlockSpec(memory_space=pltpu.HBM)] * len(inputs),
         out_specs=[vmem] * 4,
@@ -255,9 +249,9 @@
         + [
             pltpu.VMEM((basis * width, width), BF16),
             pltpu.VMEM((basis * width, width), BF16),
-            pltpu.VMEM((count // (groups * group), groups * group, basis * width), F32),
-            pltpu.VMEM((groups * width, basis * width), BF16),
-            pltpu.VMEM((groups * width, basis * width), BF16),
+            pltpu.VMEM((count, basis * width), F32),
+            pltpu.VMEM((max(chunks[0::2]) * width, basis * width), BF16),
+            pltpu.VMEM((max(chunks[1::2]) * width, basis * width), BF16),
             pltpu.VMEM((patches * stride, width), F32),
             pltpu.VMEM((strips, patches, width), F32),
             pltpu.SemaphoreType.DMA((len(inputs),)),

time: 30.2 us -> 30.2 us (level)
  no operation moved by 1% of the time
where the time goes in v3:
time: 30.2 us; the launch traced here: 30 us
  waiting for transfers between devices  11.3 us (37%)
  Pallas kernels  9.22 us (31%)
  starting transfers between devices  8.65 us (29%)
  between operations  0.66 us (2%)
    ppermute x7, waiting for transfers between devices, exchange(): lax.ppermute(x, ('patch', 'visit'), [(d, d ^ mask) for d in range(parts)])  11.3 us
    ppermute x7, starting transfers between devices, exchange(): lax.ppermute(x, ('patch', 'visit'), [(d, d ^ mask) for d in range(parts)])  8.65 us
    pallas_call x1, Pallas kernels, shards(): pl.pallas_call(partial(coadd_kernel, (patches, strips, halo, stride, grou...  8.22 us
    pallas_call x1, Pallas kernels, shards(): pl.pallas_call(partial(detect_kernel, halo), out_shape=(shape, shape), in...  1 us
  transfers between devices with their start and end apart: 7, of which 6 were waited for; matrix products, arithmetic and copies ran while one was open for 0% of the time, Pallas kernels for 0%

profile of v3, /device:TPU:0, one launch (start us, length us, event | category | flops | bytes accessed | tf_op | source)
XLA Modules:
  0.0 30.0 jit_solution(829733730624993359)
XLA Ops:
  0.6 8.2 %coadd_partials.1 = (f32[16,88,128]{2,1,0:T(8,128)S(1)}, bf16[16,88,128]{2,1,0:T(8,128)(2,1)S(1)}, bf16[128,128]{1,0:T(8,128)(2,1)S(1)}, bf16[64,128]{1,0:T(8,128)(2,1)S(1)}) custom-call(bf16[14,41]{1,0:T(8,128)(2,1)} %col_h.1, bf16[14,41]{1,0:T(8,128)(2,1)} %row_h.1, s32[1,96]{1,0:T(1,128)} %bitcast.15, s32[1,96]{1,0:T(1,128)} %bitcast.17, ...), custom_call_target="tpu_custom_call" | custom-call | tf_op jit(solution)/shard_map/coadd_partials/pallas_call | solution.py:242
  8.9 0.5 %collective-permute-start = (bf16[16,88,128]{2,1,0:T(8,128)(2,1)S(1)}, bf16[16,88,128]{2,1,0:T(8,128)(2,1)S(1)}, u32[]{:S(2)}, u32[]{:S(2)}) collective-permute-start(bf16[16,88,128]{2,1,0:T(8,128)(2,1)S(1)} %get-tuple-element.7), channel_id=1, source_target_pairs={{0,1},{1,0},{2,3},{3,2},{4,5},{5,4},{6,7},{7,6},{8,9},{9,8},{10,11... | collective-permute-start | bytes 1081352 | tf_op jit(solution)/shard_map/ppermute | solution.py:263
  9.4 1.3 %collective-permute-done = bf16[16,88,128]{2,1,0:T(8,128)(2,1)S(1)} collective-permute-done((bf16[16,88,128]{2,1,0:T(8,128)(2,1)S(1)}, bf16[16,88,128]{2,1,0:T(8,128)(2,1)S(1)}, u32[]{:S(2)}, u32[]{:S(2)}) %collective-permute-start) | collective-permute-done | bytes 360480 | tf_op jit(solution)/shard_map/ppermute | solution.py:263
  10.7 0.1 add_convert_fusion.2
  10.8 2.7 %collective-permute-start.1 = (bf16[4,88,128]{2,1,0:T(8,128)(2,1)S(1)}, bf16[4,88,128]{2,1,0:T(8,128)(2,1)S(1)}, u32[]{:S(2)}, u32[]{:S(2)}) collective-permute-start(bf16[4,88,128]{2,1,0:T(8,128)(2,1)S(1)} %get-tuple-element.12), channel_id=1, source_target_pairs={{0,3},{1,2},{2,1},{3,0},{4,7},{5,6},{6,5},{7,4},{8,11},{9,10},{10,... | collective-permute-start | bytes 270344 | tf_op jit(solution)/shard_map/ppermute | solution.py:206
  13.4 1.5 %collective-permute-start.3 = (bf16[4,88,128]{2,1,0:T(8,128)(2,1)S(1)}, bf16[4,88,128]{2,1,0:T(8,128)(2,1)S(1)}, u32[]{:S(2)}, u32[]{:S(2)}) collective-permute-start(bf16[4,88,128]{2,1,0:T(8,128)(2,1)S(1)} %get-tuple-element.13), channel_id=1, source_target_pairs={{0,5},{1,4},{2,7},{3,6},{4,1},{5,0},{6,3},{7,2},{8,13},{9,12},{10,... | collective-permute-start | bytes 270344 | tf_op jit(solution)/shard_map/ppermute | solution.py:206
  14.9 0.0 collective-permute-start.2
  14.9 1.5 %collective-permute-done.1 = bf16[4,88,128]{2,1,0:T(8,128)(2,1)S(1)} collective-permute-done((bf16[4,88,128]{2,1,0:T(8,128)(2,1)S(1)}, bf16[4,88,128]{2,1,0:T(8,128)(2,1)S(1)}, u32[]{:S(2)}, u32[]{:S(2)}) %collective-permute-start.1) | collective-permute-done | bytes 90144 | tf_op jit(solution)/shard_map/ppermute | solution.py:206
  16.4 2.9 %collective-permute-done.3 = bf16[4,88,128]{2,1,0:T(8,128)(2,1)S(1)} collective-permute-done((bf16[4,88,128]{2,1,0:T(8,128)(2,1)S(1)}, bf16[4,88,128]{2,1,0:T(8,128)(2,1)S(1)}, u32[]{:S(2)}, u32[]{:S(2)}) %collective-permute-start.3) | collective-permute-done | bytes 90144 | tf_op jit(solution)/shard_map/ppermute | solution.py:206
  19.4 1.0 %collective-permute-done.2 = bf16[4,88,128]{2,1,0:T(8,128)(2,1)S(1)} collective-permute-done((bf16[4,88,128]{2,1,0:T(8,128)(2,1)S(1)}, bf16[4,88,128]{2,1,0:T(8,128)(2,1)S(1)}, u32[]{:S(2)}, u32[]{:S(2)}) %collective-permute-start.2) | collective-permute-done | bytes 90144 | tf_op jit(solution)/shard_map/ppermute | solution.py:206
  20.4 0.1 fusion
  20.5 1.4 %collective-permute-start.6 = (bf16[88,128]{1,0:T(8,128)(2,1)S(1)}, bf16[88,128]{1,0:T(8,128)(2,1)S(1)}, u32[]{:S(2)}, u32[]{:S(2)}) collective-permute-start(bf16[88,128]{1,0:T(8,128)(2,1)S(1)} %get-tuple-element.15), channel_id=1, source_target_pairs={{0,9},{1,8},{2,11},{3,10},{4,13},{5,12},{6,15},{7,14},{8,1},{9,0},... | collective-permute-start | bytes 67592 | tf_op jit(solution)/shard_map/ppermute | solution.py:206
  21.9 2.4 %collective-permute-start.5 = (bf16[88,128]{1,0:T(8,128)(2,1)S(1)}, bf16[88,128]{1,0:T(8,128)(2,1)S(1)}, u32[]{:S(2)}, u32[]{:S(2)}) collective-permute-start(bf16[88,128]{1,0:T(8,128)(2,1)S(1)} %get-tuple-element.16), channel_id=1, source_target_pairs={{0,25},{1,24},{2,27},{3,26},{4,29},{5,28},{6,31},{7,30},{8,17},{9,... | collective-permute-start | bytes 67592 | tf_op jit(solution)/shard_map/ppermute | solution.py:206
  24.3 0.1 collective-permute-start.4
  24.5 0.0 collective-permute-done.6.refs_3_
  24.5 2.5 %collective-permute-done.5.refs_2_ = bf16[88,128]{1,0:T(8,128)(2,1)S(1)} collective-permute-done((bf16[88,128]{1,0:T(8,128)(2,1)S(1)}, bf16[88,128]{1,0:T(8,128)(2,1)S(1)}, u32[]{:S(2)}, u32[]{:S(2)}) %collective-permute-start.5) | collective-permute-done | bytes 22560 | tf_op jit(solution)/shard_map/ppermute | solution.py:206
  26.9 2.0 %collective-permute-done.4.refs_1_ = bf16[88,128]{1,0:T(8,128)(2,1)S(1)} collective-permute-done((bf16[88,128]{1,0:T(8,128)(2,1)S(1)}, bf16[88,128]{1,0:T(8,128)(2,1)S(1)}, u32[]{:S(2)}, u32[]{:S(2)}) %collective-permute-start.4) | collective-permute-done | bytes 22560 | tf_op jit(solution)/shard_map/ppermute | solution.py:206
  29.0 1.0 %detect_strip.1 = (f32[64,128]{1,0:T(8,128)}, f32[64,128]{1,0:T(8,128)}) custom-call(f32[88,128]{1,0:T(8,128)S(1)} %slice_bitcast_fusion.refs_0_, bf16[88,128]{1,0:T(8,128)(2,1)S(1)} %collective-permute-done.4.refs_1_, bf16[88,128]{1,0:T(8,128)(2,1)S(1)} %collective-permute-done.5.refs_2_, bf16[88,128]{1,0:T(8,128)(2,1)S(1)} %collective-permute-done.6.refs_3_, ...), custom_call_target="tpu_custom_call" | custom-call | tf_op jit(solution)/shard_map/detect_strip/pallas_call | solution.py:279
  (2 shorter events, 0.0 us)
Async XLA Ops:
  8.9 1.8 %collective-permute-start = (bf16[16,88,128]{2,1,0:T(8,128)(2,1)S(1)}, bf16[16,88,128]{2,1,0:T(8,128)(2,1)S(1)}, u32[]{:S(2)}, u32[]{:S(2)}) collective-permute-start(bf16[16,88,128]{2,1,0:T(8,128)(2,1)S(1)} %get-tuple-element.7), channel_id=1, source_target_pairs={{0,1},{1,0},{2,3},{3,2},{4,5},{5,4},{6,7},{7,6},{8,9},{9,8},{10,11... | collective-permute-start | bytes 1081352 | tf_op jit(solution)/shard_map/ppermute | solution.py:263
  10.8 5.7 %collective-permute-start.1 = (bf16[4,88,128]{2,1,0:T(8,128)(2,1)S(1)}, bf16[4,88,128]{2,1,0:T(8,128)(2,1)S(1)}, u32[]{:S(2)}, u32[]{:S(2)}) collective-permute-start(bf16[4,88,128]{2,1,0:T(8,128)(2,1)S(1)} %get-tuple-element.12), channel_id=1, source_target_pairs={{0,3},{1,2},{2,1},{3,0},{4,7},{5,6},{6,5},{7,4},{8,11},{9,10},{10,... | collective-permute-start | bytes 270344 | tf_op jit(solution)/shard_map/ppermute | solution.py:206
  13.4 5.9 %collective-permute-start.3 = (bf16[4,88,128]{2,1,0:T(8,128)(2,1)S(1)}, bf16[4,88,128]{2,1,0:T(8,128)(2,1)S(1)}, u32[]{:S(2)}, u32[]{:S(2)}) collective-permute-start(bf16[4,88,128]{2,1,0:T(8,128)(2,1)S(1)} %get-tuple-element.13), channel_id=1, source_target_pairs={{0,5},{1,4},{2,7},{3,6},{4,1},{5,0},{6,3},{7,2},{8,13},{9,12},{10,... | collective-permute-start | bytes 270344 | tf_op jit(solution)/shard_map/ppermute | solution.py:206
  14.9 5.5 %collective-permute-start.2 = (bf16[4,88,128]{2,1,0:T(8,128)(2,1)S(1)}, bf16[4,88,128]{2,1,0:T(8,128)(2,1)S(1)}, u32[]{:S(2)}, u32[]{:S(2)}) collective-permute-start(bf16[4,88,128]{2,1,0:T(8,128)(2,1)S(1)} %get-tuple-element.14), channel_id=1, source_target_pairs={{0,7},{1,6},{2,5},{3,4},{4,3},{5,2},{6,1},{7,0},{8,15},{9,14},{10,... | collective-permute-start | bytes 270344 | tf_op jit(solution)/shard_map/ppermute | solution.py:206
  20.5 4.0 %collective-permute-start.6 = (bf16[88,128]{1,0:T(8,128)(2,1)S(1)}, bf16[88,128]{1,0:T(8,128)(2,1)S(1)}, u32[]{:S(2)}, u32[]{:S(2)}) collective-permute-start(bf16[88,128]{1,0:T(8,128)(2,1)S(1)} %get-tuple-element.15), channel_id=1, source_target_pairs={{0,9},{1,8},{2,11},{3,10},{4,13},{5,12},{6,15},{7,14},{8,1},{9,0},... | collective-permute-start | bytes 67592 | tf_op jit(solution)/shard_map/ppermute | solution.py:206
  21.9 5.0 %collective-permute-start.5 = (bf16[88,128]{1,0:T(8,128)(2,1)S(1)}, bf16[88,128]{1,0:T(8,128)(2,1)S(1)}, u32[]{:S(2)}, u32[]{:S(2)}) collective-permute-start(bf16[88,128]{1,0:T(8,128)(2,1)S(1)} %get-tuple-element.16), channel_id=1, source_target_pairs={{0,25},{1,24},{2,27},{3,26},{4,29},{5,28},{6,31},{7,30},{8,17},{9,... | collective-permute-start | bytes 67592 | tf_op jit(solution)/shard_map/ppermute | solution.py:206
  24.3 4.6 %collective-permute-start.4 = (bf16[88,128]{1,0:T(8,128)(2,1)S(1)}, bf16[88,128]{1,0:T(8,128)(2,1)S(1)}, u32[]{:S(2)}, u32[]{:S(2)}) collective-permute-start(bf16[88,128]{1,0:T(8,128)(2,1)S(1)} %get-tuple-element.17), channel_id=1, source_target_pairs={{0,17},{1,16},{2,19},{3,18},{4,21},{5,20},{6,23},{7,22},{8,25},{9,... | collective-permute-start | bytes 67592 | tf_op jit(solution)/shard_map/ppermute | solution.py:206

commit v4 on v3

--- a/solution.py
+++ b/solution.py
@@ -269,12 +269,12 @@
             kept = kept[:left] + given[:left].astype(F32)
         given = exchange(sent, mask)
     sums = [kept[4 * k:4 * k + 4] + given[4 * k:4 * k + 4].astype(F32) for k in range(4)]
-    terms = exchange_direct(sums, partial(direct_mask, halved, 0), (1, 3, 2))
+    terms = exchange_direct(sums, partial(direct_mask, halved, 0), (3, 1, 2))
     total = terms[0]
     for term in terms[1:]:
         total = total + term.astype(F32)
     total = [total[k] for k in range(4)]
-    terms = exchange_direct(total, partial(direct_mask, halved, 1), (2, 3, 1))
+    terms = exchange_direct(total, partial(direct_mask, halved, 1), (3, 2, 1))
     shape = jax.ShapeDtypeStruct((strip, width), F32)
     return pl.pallas_call(
         partial(detect_kernel, halo),

time: 30.2 us -> 30.2 us (level)
  no operation moved by 1% of the time
where the time goes in v4:
time: 30.2 us; the launch traced here: 30 us
  waiting for transfers between devices  11.2 us (37%)
  Pallas kernels  9.22 us (31%)
  starting transfers between devices  8.81 us (29%)
  between operations  0.66 us (2%)
    ppermute x7, waiting for transfers between devices, exchange(): lax.ppermute(x, ('patch', 'visit'), [(d, d ^ mask) for d in range(parts)])  11.2 us
    ppermute x7, starting transfers between devices, exchange(): lax.ppermute(x, ('patch', 'visit'), [(d, d ^ mask) for d in range(parts)])  8.81 us
    pallas_call x1, Pallas kernels, shards(): pl.pallas_call(partial(coadd_kernel, (patches, strips, halo, stride, grou...  8.22 us
    pallas_call x1, Pallas kernels, shards(): pl.pallas_call(partial(detect_kernel, halo), out_shape=(shape, shape), in...  1 us
  transfers between devices with their start and end apart: 7, of which 6 were waited for; matrix products, arithmetic and copies ran while one was open for 0% of the time, Pallas kernels for 0%

profile of v4, /device:TPU:0, one launch (start us, length us, event | category | flops | bytes accessed | tf_op | source)
XLA Modules:
  0.0 30.0 jit_solution(10955727357042417983)
XLA Ops:
  0.6 8.2 %coadd_partials.1 = (f32[16,88,128]{2,1,0:T(8,128)S(1)}, bf16[16,88,128]{2,1,0:T(8,128)(2,1)S(1)}, bf16[128,128]{1,0:T(8,128)(2,1)S(1)}, bf16[64,128]{1,0:T(8,128)(2,1)S(1)}) custom-call(bf16[14,41]{1,0:T(8,128)(2,1)} %col_h.1, bf16[14,41]{1,0:T(8,128)(2,1)} %row_h.1, s32[1,96]{1,0:T(1,128)} %bitcast.15, s32[1,96]{1,0:T(1,128)} %bitcast.17, ...), custom_call_target="tpu_custom_call" | custom-call | tf_op jit(solution)/shard_map/coadd_partials/pallas_call | solution.py:242
  8.9 0.5 %collective-permute-start = (bf16[16,88,128]{2,1,0:T(8,128)(2,1)S(1)}, bf16[16,88,128]{2,1,0:T(8,128)(2,1)S(1)}, u32[]{:S(2)}, u32[]{:S(2)}) collective-permute-start(bf16[16,88,128]{2,1,0:T(8,128)(2,1)S(1)} %get-tuple-element.7), channel_id=1, source_target_pairs={{0,1},{1,0},{2,3},{3,2},{4,5},{5,4},{6,7},{7,6},{8,9},{9,8},{10,11... | collective-permute-start | bytes 1081352 | tf_op jit(solution)/shard_map/ppermute | solution.py:263
  9.4 1.3 %collective-permute-done = bf16[16,88,128]{2,1,0:T(8,128)(2,1)S(1)} collective-permute-done((bf16[16,88,128]{2,1,0:T(8,128)(2,1)S(1)}, bf16[16,88,128]{2,1,0:T(8,128)(2,1)S(1)}, u32[]{:S(2)}, u32[]{:S(2)}) %collective-permute-start) | collective-permute-done | bytes 360480 | tf_op jit(solution)/shard_map/ppermute | solution.py:263
  10.7 0.1 add_convert_fusion.2
  10.8 3.6 %collective-permute-start.1 = (bf16[4,88,128]{2,1,0:T(8,128)(2,1)S(1)}, bf16[4,88,128]{2,1,0:T(8,128)(2,1)S(1)}, u32[]{:S(2)}, u32[]{:S(2)}) collective-permute-start(bf16[4,88,128]{2,1,0:T(8,128)(2,1)S(1)} %get-tuple-element.12), channel_id=1, source_target_pairs={{0,7},{1,6},{2,5},{3,4},{4,3},{5,2},{6,1},{7,0},{8,15},{9,14},{10,... | collective-permute-start | bytes 270344 | tf_op jit(solution)/shard_map/ppermute | solution.py:206
  14.4 0.5 %collective-permute-start.3 = (bf16[4,88,128]{2,1,0:T(8,128)(2,1)S(1)}, bf16[4,88,128]{2,1,0:T(8,128)(2,1)S(1)}, u32[]{:S(2)}, u32[]{:S(2)}) collective-permute-start(bf16[4,88,128]{2,1,0:T(8,128)(2,1)S(1)} %get-tuple-element.13), channel_id=1, source_target_pairs={{0,5},{1,4},{2,7},{3,6},{4,1},{5,0},{6,3},{7,2},{8,13},{9,12},{10,... | collective-permute-start | bytes 270344 | tf_op jit(solution)/shard_map/ppermute | solution.py:206
  14.9 0.1 collective-permute-start.2
  15.0 2.4 %collective-permute-done.1 = bf16[4,88,128]{2,1,0:T(8,128)(2,1)S(1)} collective-permute-done((bf16[4,88,128]{2,1,0:T(8,128)(2,1)S(1)}, bf16[4,88,128]{2,1,0:T(8,128)(2,1)S(1)}, u32[]{:S(2)}, u32[]{:S(2)}) %collective-permute-start.1) | collective-permute-done | bytes 90144 | tf_op jit(solution)/shard_map/ppermute | solution.py:206
  17.4 1.8 %collective-permute-done.3 = bf16[4,88,128]{2,1,0:T(8,128)(2,1)S(1)} collective-permute-done((bf16[4,88,128]{2,1,0:T(8,128)(2,1)S(1)}, bf16[4,88,128]{2,1,0:T(8,128)(2,1)S(1)}, u32[]{:S(2)}, u32[]{:S(2)}) %collective-permute-start.3) | collective-permute-done | bytes 90144 | tf_op jit(solution)/shard_map/ppermute | solution.py:206
  19.2 0.6 %collective-permute-done.2 = bf16[4,88,128]{2,1,0:T(8,128)(2,1)S(1)} collective-permute-done((bf16[4,88,128]{2,1,0:T(8,128)(2,1)S(1)}, bf16[4,88,128]{2,1,0:T(8,128)(2,1)S(1)}, u32[]{:S(2)}, u32[]{:S(2)}) %collective-permute-start.2) | collective-permute-done | bytes 90144 | tf_op jit(solution)/shard_map/ppermute | solution.py:206
  19.8 0.1 fusion
  19.9 1.4 %collective-permute-start.6 = (bf16[88,128]{1,0:T(8,128)(2,1)S(1)}, bf16[88,128]{1,0:T(8,128)(2,1)S(1)}, u32[]{:S(2)}, u32[]{:S(2)}) collective-permute-start(bf16[88,128]{1,0:T(8,128)(2,1)S(1)} %get-tuple-element.15), channel_id=1, source_target_pairs={{0,9},{1,8},{2,11},{3,10},{4,13},{5,12},{6,15},{7,14},{8,1},{9,0},... | collective-permute-start | bytes 67592 | tf_op jit(solution)/shard_map/ppermute | solution.py:206
  21.3 2.6 %collective-permute-start.5 = (bf16[88,128]{1,0:T(8,128)(2,1)S(1)}, bf16[88,128]{1,0:T(8,128)(2,1)S(1)}, u32[]{:S(2)}, u32[]{:S(2)}) collective-permute-start(bf16[88,128]{1,0:T(8,128)(2,1)S(1)} %get-tuple-element.16), channel_id=1, source_target_pairs={{0,17},{1,16},{2,19},{3,18},{4,21},{5,20},{6,23},{7,22},{8,25},{9,... | collective-permute-start | bytes 67592 | tf_op jit(solution)/shard_map/ppermute | solution.py:206
  24.0 0.0 collective-permute-start.4
  24.0 0.0 collective-permute-done.6.refs_3_
  24.0 1.7 %collective-permute-done.5.refs_2_ = bf16[88,128]{1,0:T(8,128)(2,1)S(1)} collective-permute-done((bf16[88,128]{1,0:T(8,128)(2,1)S(1)}, bf16[88,128]{1,0:T(8,128)(2,1)S(1)}, u32[]{:S(2)}, u32[]{:S(2)}) %collective-permute-start.5) | collective-permute-done | bytes 22560 | tf_op jit(solution)/shard_map/ppermute | solution.py:206
  25.7 3.3 %collective-permute-done.4.refs_1_ = bf16[88,128]{1,0:T(8,128)(2,1)S(1)} collective-permute-done((bf16[88,128]{1,0:T(8,128)(2,1)S(1)}, bf16[88,128]{1,0:T(8,128)(2,1)S(1)}, u32[]{:S(2)}, u32[]{:S(2)}) %collective-permute-start.4) | collective-permute-done | bytes 22560 | tf_op jit(solution)/shard_map/ppermute | solution.py:206
  29.0 1.0 %detect_strip.1 = (f32[64,128]{1,0:T(8,128)}, f32[64,128]{1,0:T(8,128)}) custom-call(f32[88,128]{1,0:T(8,128)S(1)} %slice_bitcast_fusion.refs_0_, bf16[88,128]{1,0:T(8,128)(2,1)S(1)} %collective-permute-done.4.refs_1_, bf16[88,128]{1,0:T(8,128)(2,1)S(1)} %collective-permute-done.5.refs_2_, bf16[88,128]{1,0:T(8,128)(2,1)S(1)} %collective-permute-done.6.refs_3_, ...), custom_call_target="tpu_custom_call" | custom-call | tf_op jit(solution)/shard_map/detect_strip/pallas_call | solution.py:279
  (2 shorter events, 0.0 us)
Async XLA Ops:
  8.9 1.8 %collective-permute-start = (bf16[16,88,128]{2,1,0:T(8,128)(2,1)S(1)}, bf16[16,88,128]{2,1,0:T(8,128)(2,1)S(1)}, u32[]{:S(2)}, u32[]{:S(2)}) collective-permute-start(bf16[16,88,128]{2,1,0:T(8,128)(2,1)S(1)} %get-tuple-element.7), channel_id=1, source_target_pairs={{0,1},{1,0},{2,3},{3,2},{4,5},{5,4},{6,7},{7,6},{8,9},{9,8},{10,11... | collective-permute-start | bytes 1081352 | tf_op jit(solution)/shard_map/ppermute | solution.py:263
  10.8 6.7 %collective-permute-start.1 = (bf16[4,88,128]{2,1,0:T(8,128)(2,1)S(1)}, bf16[4,88,128]{2,1,0:T(8,128)(2,1)S(1)}, u32[]{:S(2)}, u32[]{:S(2)}) collective-permute-start(bf16[4,88,128]{2,1,0:T(8,128)(2,1)S(1)} %get-tuple-element.12), channel_id=1, source_target_pairs={{0,7},{1,6},{2,5},{3,4},{4,3},{5,2},{6,1},{7,0},{8,15},{9,14},{10,... | collective-permute-start | bytes 270344 | tf_op jit(solution)/shard_map/ppermute | solution.py:206
  14.4 4.8 %collective-permute-start.3 = (bf16[4,88,128]{2,1,0:T(8,128)(2,1)S(1)}, bf16[4,88,128]{2,1,0:T(8,128)(2,1)S(1)}, u32[]{:S(2)}, u32[]{:S(2)}) collective-permute-start(bf16[4,88,128]{2,1,0:T(8,128)(2,1)S(1)} %get-tuple-element.13), channel_id=1, source_target_pairs={{0,5},{1,4},{2,7},{3,6},{4,1},{5,0},{6,3},{7,2},{8,13},{9,12},{10,... | collective-permute-start | bytes 270344 | tf_op jit(solution)/shard_map/ppermute | solution.py:206
  14.9 5.0 %collective-permute-start.2 = (bf16[4,88,128]{2,1,0:T(8,128)(2,1)S(1)}, bf16[4,88,128]{2,1,0:T(8,128)(2,1)S(1)}, u32[]{:S(2)}, u32[]{:S(2)}) collective-permute-start(bf16[4,88,128]{2,1,0:T(8,128)(2,1)S(1)} %get-tuple-element.14), channel_id=1, source_target_pairs={{0,3},{1,2},{2,1},{3,0},{4,7},{5,6},{6,5},{7,4},{8,11},{9,10},{10,... | collective-permute-start | bytes 270344 | tf_op jit(solution)/shard_map/ppermute | solution.py:206
  19.9 4.1 %collective-permute-start.6 = (bf16[88,128]{1,0:T(8,128)(2,1)S(1)}, bf16[88,128]{1,0:T(8,128)(2,1)S(1)}, u32[]{:S(2)}, u32[]{:S(2)}) collective-permute-start(bf16[88,128]{1,0:T(8,128)(2,1)S(1)} %get-tuple-element.15), channel_id=1, source_target_pairs={{0,9},{1,8},{2,11},{3,10},{4,13},{5,12},{6,15},{7,14},{8,1},{9,0},... | collective-permute-start | bytes 67592 | tf_op jit(solution)/shard_map/ppermute | solution.py:206
  21.3 4.3 %collective-permute-start.5 = (bf16[88,128]{1,0:T(8,128)(2,1)S(1)}, bf16[88,128]{1,0:T(8,128)(2,1)S(1)}, u32[]{:S(2)}, u32[]{:S(2)}) collective-permute-start(bf16[88,128]{1,0:T(8,128)(2,1)S(1)} %get-tuple-element.16), channel_id=1, source_target_pairs={{0,17},{1,16},{2,19},{3,18},{4,21},{5,20},{6,23},{7,22},{8,25},{9,... | collective-permute-start | bytes 67592 | tf_op jit(solution)/shard_map/ppermute | solution.py:206
  24.0 5.0 %collective-permute-start.4 = (bf16[88,128]{1,0:T(8,128)(2,1)S(1)}, bf16[88,128]{1,0:T(8,128)(2,1)S(1)}, u32[]{:S(2)}, u32[]{:S(2)}) collective-permute-start(bf16[88,128]{1,0:T(8,128)(2,1)S(1)} %get-tuple-element.17), channel_id=1, source_target_pairs={{0,25},{1,24},{2,27},{3,26},{4,29},{5,28},{6,31},{7,30},{8,17},{9,... | collective-permute-start | bytes 67592 | tf_op jit(solution)/shard_map/ppermute | solution.py:206

commit v5 on v4

--- a/solution.py
+++ b/solution.py
@@ -274,7 +274,7 @@
     for term in terms[1:]:
         total = total + term.astype(F32)
     total = [total[k] for k in range(4)]
-    terms = exchange_direct(total, partial(direct_mask, halved, 1), (3, 2, 1))
+    terms = exchange_direct(total, partial(direct_mask, halved, 1), (1, 2, 3))
     shape = jax.ShapeDtypeStruct((strip, width), F32)
     return pl.pallas_call(
         partial(detect_kernel, halo),

time: 30.2 us -> 28.7 us (0.950)
  waiting for transfers between devices: 11.2 us -> 9.62 us
    ppermute x7, waiting for transfers between devices: 11.2 us -> 9.62 us  [exchange(): lax.ppermute(x, ('patch', 'visit'), [(d, d ^ mask) for d in range(parts)])]
where the time goes in v5:
time: 28.7 us; the launch traced here: 28.5 us
  waiting for transfers between devices  9.62 us (34%)
  Pallas kernels  9.23 us (32%)
  starting transfers between devices  8.85 us (31%)
  between operations  0.66 us (2%)
    ppermute x7, waiting for transfers between devices, exchange(): lax.ppermute(x, ('patch', 'visit'), [(d, d ^ mask) for d in range(parts)])  9.62 us
    ppermute x7, starting transfers between devices, exchange(): lax.ppermute(x, ('patch', 'visit'), [(d, d ^ mask) for d in range(parts)])  8.85 us
    pallas_call x1, Pallas kernels, shards(): pl.pallas_call(partial(coadd_kernel, (patches, strips, halo, stride, grou...  8.23 us
    pallas_call x1, Pallas kernels, shards(): pl.pallas_call(partial(detect_kernel, halo), out_shape=(shape, shape), in...  1 us
  transfers between devices with their start and end apart: 7, of which 6 were waited for; matrix products, arithmetic and copies ran while one was open for 0% of the time, Pallas kernels for 0%

profile of v5, /device:TPU:0, one launch (start us, length us, event | category | flops | bytes accessed | tf_op | source)
XLA Modules:
  0.0 28.5 jit_solution(13923571950697381066)
XLA Ops:
  0.6 8.2 %coadd_partials.1 = (f32[16,88,128]{2,1,0:T(8,128)S(1)}, bf16[16,88,128]{2,1,0:T(8,128)(2,1)S(1)}, bf16[128,128]{1,0:T(8,128)(2,1)S(1)}, bf16[64,128]{1,0:T(8,128)(2,1)S(1)}) custom-call(bf16[14,41]{1,0:T(8,128)(2,1)} %col_h.1, bf16[14,41]{1,0:T(8,128)(2,1)} %row_h.1, s32[1,96]{1,0:T(1,128)} %bitcast.15, s32[1,96]{1,0:T(1,128)} %bitcast.17, ...), custom_call_target="tpu_custom_call" | custom-call | tf_op jit(solution)/shard_map/coadd_partials/pallas_call | solution.py:242
  8.9 0.5 %collective-permute-start = (bf16[16,88,128]{2,1,0:T(8,128)(2,1)S(1)}, bf16[16,88,128]{2,1,0:T(8,128)(2,1)S(1)}, u32[]{:S(2)}, u32[]{:S(2)}) collective-permute-start(bf16[16,88,128]{2,1,0:T(8,128)(2,1)S(1)} %get-tuple-element.7), channel_id=1, source_target_pairs={{0,1},{1,0},{2,3},{3,2},{4,5},{5,4},{6,7},{7,6},{8,9},{9,8},{10,11... | collective-permute-start | bytes 1081352 | tf_op jit(solution)/shard_map/ppermute | solution.py:263
  9.4 1.3 %collective-permute-done = bf16[16,88,128]{2,1,0:T(8,128)(2,1)S(1)} collective-permute-done((bf16[16,88,128]{2,1,0:T(8,128)(2,1)S(1)}, bf16[16,88,128]{2,1,0:T(8,128)(2,1)S(1)}, u32[]{:S(2)}, u32[]{:S(2)}) %collective-permute-start) | collective-permute-done | bytes 360480 | tf_op jit(solution)/shard_map/ppermute | solution.py:263
  10.7 0.1 add_convert_fusion.2
  10.8 3.6 %collective-permute-start.1 = (bf16[4,88,128]{2,1,0:T(8,128)(2,1)S(1)}, bf16[4,88,128]{2,1,0:T(8,128)(2,1)S(1)}, u32[]{:S(2)}, u32[]{:S(2)}) collective-permute-start(bf16[4,88,128]{2,1,0:T(8,128)(2,1)S(1)} %get-tuple-element.12), channel_id=1, source_target_pairs={{0,7},{1,6},{2,5},{3,4},{4,3},{5,2},{6,1},{7,0},{8,15},{9,14},{10,... | collective-permute-start | bytes 270344 | tf_op jit(solution)/shard_map/ppermute | solution.py:206
  14.4 0.5 %collective-permute-start.3 = (bf16[4,88,128]{2,1,0:T(8,128)(2,1)S(1)}, bf16[4,88,128]{2,1,0:T(8,128)(2,1)S(1)}, u32[]{:S(2)}, u32[]{:S(2)}) collective-permute-start(bf16[4,88,128]{2,1,0:T(8,128)(2,1)S(1)} %get-tuple-element.13), channel_id=1, source_target_pairs={{0,5},{1,4},{2,7},{3,6},{4,1},{5,0},{6,3},{7,2},{8,13},{9,12},{10,... | collective-permute-start | bytes 270344 | tf_op jit(solution)/shard_map/ppermute | solution.py:206
  14.9 0.1 collective-permute-start.2
  15.0 2.4 %collective-permute-done.1 = bf16[4,88,128]{2,1,0:T(8,128)(2,1)S(1)} collective-permute-done((bf16[4,88,128]{2,1,0:T(8,128)(2,1)S(1)}, bf16[4,88,128]{2,1,0:T(8,128)(2,1)S(1)}, u32[]{:S(2)}, u32[]{:S(2)}) %collective-permute-start.1) | collective-permute-done | bytes 90144 | tf_op jit(solution)/shard_map/ppermute | solution.py:206
  17.4 1.8 %collective-permute-done.3 = bf16[4,88,128]{2,1,0:T(8,128)(2,1)S(1)} collective-permute-done((bf16[4,88,128]{2,1,0:T(8,128)(2,1)S(1)}, bf16[4,88,128]{2,1,0:T(8,128)(2,1)S(1)}, u32[]{:S(2)}, u32[]{:S(2)}) %collective-permute-start.3) | collective-permute-done | bytes 90144 | tf_op jit(solution)/shard_map/ppermute | solution.py:206
  19.2 0.6 %collective-permute-done.2 = bf16[4,88,128]{2,1,0:T(8,128)(2,1)S(1)} collective-permute-done((bf16[4,88,128]{2,1,0:T(8,128)(2,1)S(1)}, bf16[4,88,128]{2,1,0:T(8,128)(2,1)S(1)}, u32[]{:S(2)}, u32[]{:S(2)}) %collective-permute-start.2) | collective-permute-done | bytes 90144 | tf_op jit(solution)/shard_map/ppermute | solution.py:206
  19.8 0.1 fusion
  19.9 3.5 %collective-permute-start.6 = (bf16[88,128]{1,0:T(8,128)(2,1)S(1)}, bf16[88,128]{1,0:T(8,128)(2,1)S(1)}, u32[]{:S(2)}, u32[]{:S(2)}) collective-permute-start(bf16[88,128]{1,0:T(8,128)(2,1)S(1)} %get-tuple-element.15), channel_id=1, source_target_pairs={{0,25},{1,24},{2,27},{3,26},{4,29},{5,28},{6,31},{7,30},{8,17},{9,... | collective-permute-start | bytes 67592 | tf_op jit(solution)/shard_map/ppermute | solution.py:206
  23.4 0.0 collective-permute-start.5
  23.4 0.6 %collective-permute-start.4 = (bf16[88,128]{1,0:T(8,128)(2,1)S(1)}, bf16[88,128]{1,0:T(8,128)(2,1)S(1)}, u32[]{:S(2)}, u32[]{:S(2)}) collective-permute-start(bf16[88,128]{1,0:T(8,128)(2,1)S(1)} %get-tuple-element.17), channel_id=1, source_target_pairs={{0,9},{1,8},{2,11},{3,10},{4,13},{5,12},{6,15},{7,14},{8,1},{9,0},... | collective-permute-start | bytes 67592 | tf_op jit(solution)/shard_map/ppermute | solution.py:206
  24.0 1.0 %collective-permute-done.6.refs_3_ = bf16[88,128]{1,0:T(8,128)(2,1)S(1)} collective-permute-done((bf16[88,128]{1,0:T(8,128)(2,1)S(1)}, bf16[88,128]{1,0:T(8,128)(2,1)S(1)}, u32[]{:S(2)}, u32[]{:S(2)}) %collective-permute-start.6) | collective-permute-done | bytes 22560 | tf_op jit(solution)/shard_map/ppermute | solution.py:206
  25.0 2.5 %collective-permute-done.5.refs_2_ = bf16[88,128]{1,0:T(8,128)(2,1)S(1)} collective-permute-done((bf16[88,128]{1,0:T(8,128)(2,1)S(1)}, bf16[88,128]{1,0:T(8,128)(2,1)S(1)}, u32[]{:S(2)}, u32[]{:S(2)}) %collective-permute-start.5) | collective-permute-done | bytes 22560 | tf_op jit(solution)/shard_map/ppermute | solution.py:206
  27.5 0.0 collective-permute-done.4.refs_1_
  27.5 1.0 %detect_strip.1 = (f32[64,128]{1,0:T(8,128)}, f32[64,128]{1,0:T(8,128)}) custom-call(f32[88,128]{1,0:T(8,128)S(1)} %slice_bitcast_fusion.refs_0_, bf16[88,128]{1,0:T(8,128)(2,1)S(1)} %collective-permute-done.4.refs_1_, bf16[88,128]{1,0:T(8,128)(2,1)S(1)} %collective-permute-done.5.refs_2_, bf16[88,128]{1,0:T(8,128)(2,1)S(1)} %collective-permute-done.6.refs_3_, ...), custom_call_target="tpu_custom_call" | custom-call | tf_op jit(solution)/shard_map/detect_strip/pallas_call | solution.py:279
  (2 shorter events, 0.0 us)
Async XLA Ops:
  8.9 1.8 %collective-permute-start = (bf16[16,88,128]{2,1,0:T(8,128)(2,1)S(1)}, bf16[16,88,128]{2,1,0:T(8,128)(2,1)S(1)}, u32[]{:S(2)}, u32[]{:S(2)}) collective-permute-start(bf16[16,88,128]{2,1,0:T(8,128)(2,1)S(1)} %get-tuple-element.7), channel_id=1, source_target_pairs={{0,1},{1,0},{2,3},{3,2},{4,5},{5,4},{6,7},{7,6},{8,9},{9,8},{10,11... | collective-permute-start | bytes 1081352 | tf_op jit(solution)/shard_map/ppermute | solution.py:263
  10.8 6.7 %collective-permute-start.1 = (bf16[4,88,128]{2,1,0:T(8,128)(2,1)S(1)}, bf16[4,88,128]{2,1,0:T(8,128)(2,1)S(1)}, u32[]{:S(2)}, u32[]{:S(2)}) collective-permute-start(bf16[4,88,128]{2,1,0:T(8,128)(2,1)S(1)} %get-tuple-element.12), channel_id=1, source_target_pairs={{0,7},{1,6},{2,5},{3,4},{4,3},{5,2},{6,1},{7,0},{8,15},{9,14},{10,... | collective-permute-start | bytes 270344 | tf_op jit(solution)/shard_map/ppermute | solution.py:206
  14.4 4.8 %collective-permute-start.3 = (bf16[4,88,128]{2,1,0:T(8,128)(2,1)S(1)}, bf16[4,88,128]{2,1,0:T(8,128)(2,1)S(1)}, u32[]{:S(2)}, u32[]{:S(2)}) collective-permute-start(bf16[4,88,128]{2,1,0:T(8,128)(2,1)S(1)} %get-tuple-element.13), channel_id=1, source_target_pairs={{0,5},{1,4},{2,7},{3,6},{4,1},{5,0},{6,3},{7,2},{8,13},{9,12},{10,... | collective-permute-start | bytes 270344 | tf_op jit(solution)/shard_map/ppermute | solution.py:206
  14.9 5.0 %collective-permute-start.2 = (bf16[4,88,128]{2,1,0:T(8,128)(2,1)S(1)}, bf16[4,88,128]{2,1,0:T(8,128)(2,1)S(1)}, u32[]{:S(2)}, u32[]{:S(2)}) collective-permute-start(bf16[4,88,128]{2,1,0:T(8,128)(2,1)S(1)} %get-tuple-element.14), channel_id=1, source_target_pairs={{0,3},{1,2},{2,1},{3,0},{4,7},{5,6},{6,5},{7,4},{8,11},{9,10},{10,... | collective-permute-start | bytes 270344 | tf_op jit(solution)/shard_map/ppermute | solution.py:206
  19.9 5.1 %collective-permute-start.6 = (bf16[88,128]{1,0:T(8,128)(2,1)S(1)}, bf16[88,128]{1,0:T(8,128)(2,1)S(1)}, u32[]{:S(2)}, u32[]{:S(2)}) collective-permute-start(bf16[88,128]{1,0:T(8,128)(2,1)S(1)} %get-tuple-element.15), channel_id=1, source_target_pairs={{0,25},{1,24},{2,27},{3,26},{4,29},{5,28},{6,31},{7,30},{8,17},{9,... | collective-permute-start | bytes 67592 | tf_op jit(solution)/shard_map/ppermute | solution.py:206
  23.4 4.1 %collective-permute-start.5 = (bf16[88,128]{1,0:T(8,128)(2,1)S(1)}, bf16[88,128]{1,0:T(8,128)(2,1)S(1)}, u32[]{:S(2)}, u32[]{:S(2)}) collective-permute-start(bf16[88,128]{1,0:T(8,128)(2,1)S(1)} %get-tuple-element.16), channel_id=1, source_target_pairs={{0,17},{1,16},{2,19},{3,18},{4,21},{5,20},{6,23},{7,22},{8,25},{9,... | collective-permute-start | bytes 67592 | tf_op jit(solution)/shard_map/ppermute | solution.py:206
  23.4 4.1 %collective-permute-start.4 = (bf16[88,128]{1,0:T(8,128)(2,1)S(1)}, bf16[88,128]{1,0:T(8,128)(2,1)S(1)}, u32[]{:S(2)}, u32[]{:S(2)}) collective-permute-start(bf16[88,128]{1,0:T(8,128)(2,1)S(1)} %get-tuple-element.17), channel_id=1, source_target_pairs={{0,9},{1,8},{2,11},{3,10},{4,13},{5,12},{6,15},{7,14},{8,1},{9,0},... | collective-permute-start | bytes 67592 | tf_op jit(solution)/shard_map/ppermute | solution.py:206
